TPU v7x, 1024 devices: a whole 4x8x16 slice. The times are simulated.
1024 devices in a mesh: stream: 32 (over z_hi, y, core), trans: 32 (over x, z_lo).
Axes of the slice: x: 4, y: 8, z: 16 (z_hi: 2, z_lo: 8; z = z_hi * 8 + z_lo), core: 2. Of those that a mesh axis runs over, the one named last changes fastest.
Arguments:
- populations: float32 [19, 64, 256, 128], P(None, 'stream', 'trans'), may hold values from 0.01 to 0.2
- solid: int32 [64, 256, 128], P('stream', 'trans'), may hold values 0 or 1
- support: int32 [131072], P(('stream', 'trans')), may hold values from 0 to 32638, as said below
- fractions: float32 [3, 131072], P(None, ('stream', 'trans')), may hold values from 0 to 1
- target: float32 [3, 131072], P(None, ('stream', 'trans')), may hold values from -0.1 to 0.1
- area: float32 [131072], P(('stream', 'trans')), may hold values from 1 to 4
Outputs:
- new_populations: float32 [19, 64, 256, 128], P(None, 'stream', 'trans')
- marker_force: float32 [3, 131072], P(None, ('stream', 'trans'))
Inputs may be any that keep to these rules, and one draw needn't show every extreme that they name: support[m] = (a * 256 + b) * 128 + e with a = 0 counted inside marker m's streamwise slab m // (128 * 32) (each cube spans the slab's two planes), 0 <= b <= 256 - 2 over the whole first transverse dimension and 0 <= e <= 126.
All inputs are finite; a program needn't handle non-finite values. No bound on the sum of `solid` on one device may be relied on, other than what follows from the above.
Results may differ from a plain program's by a relative error of at most 0.0003.
Values sent between devices are 32-bit elements; how exact they have to be, the bound alone decides.
A program may use at most 32 MiB of HBM per device.

v0:
```python
import math

import jax
import jax.numpy as jnp
from jax import lax
from jax.sharding import PartitionSpec as P

STEPS = 2


velocity_table = (
    (0, 0, 0),
    (1, 0, 0),
    (-1, 0, 0),
    (0, 1, 0),
    (0, -1, 0),
    (0, 0, 1),
    (0, 0, -1),
    (1, 1, 0),
    (-1, -1, 0),
    (1, -1, 0),
    (-1, 1, 0),
    (1, 0, 1),
    (-1, 0, -1),
    (1, 0, -1),
    (-1, 0, 1),
    (0, 1, 1),
    (0, -1, -1),
    (0, 1, -1),
    (0, -1, 1),
)
weight_table = (1.0 / 3.0,) + (1.0 / 18.0,) * 6 + (1.0 / 36.0,) * 12
opposite = (0, 2, 1, 4, 3, 6, 5, 8, 7, 10, 9, 12, 11, 14, 13, 16, 15, 18, 17)
relax_base = 0.8
smagorinsky = 0.17


def extended(block, sides, width):
    for axis, dim in sides:
        count = lax.axis_size(axis)
        forward = [(i, i + 1) for i in range(count - 1)]
        forward.append((count - 1, 0))
        backward = [(target, source) for source, target in forward]
        low = lax.ppermute(
            lax.slice_in_dim(block, block.shape[dim] - width, None, axis=dim), axis, forward
        )
        high = lax.ppermute(lax.slice_in_dim(block, 0, width, axis=dim), axis, backward)
        block = jnp.concatenate([low, block, high], axis=dim)
    return block


def signed_sum(factors, values):
    running = None
    for factor, value in zip(factors, values):
        if factor != 0:
            signed_term = value if factor > 0 else -value
            running = signed_term if running is None else running + signed_term
    return 0.0 if running is None else running


def moments(fields):
    density = fields[0]
    for member in range(1, 19):
        density = density + fields[member]
    momenta = []
    for dimension in range(3):
        momenta.append(
            signed_sum(
                [velocity_table[member][dimension] for member in range(19)],
                [fields[member] for member in range(19)],
            )
        )
    return (density, momenta)


def collide(fields, density, momenta, forcing, solid):
    velocity = [(momenta[dimension] + 0.5 * forcing[dimension]) / density for dimension in range(3)]
    square = velocity[0] * velocity[0] + velocity[1] * velocity[1] + velocity[2] * velocity[2]
    force_along = velocity[0] * forcing[0] + velocity[1] * forcing[1] + velocity[2] * forcing[2]
    projections = []
    nonequil = []
    for member in range(19):
        projected = signed_sum(velocity_table[member], velocity)
        equilibrium = (
            weight_table[member]
            * density
            * (1.0 + 3.0 * projected + 4.5 * projected * projected - 1.5 * square)
        )
        projections.append(projected)
        nonequil.append(fields[member] - equilibrium)
    magnitude_square = 0.0
    for first, second in ((0, 0), (1, 1), (2, 2), (0, 1), (0, 2), (1, 2)):
        component = signed_sum(
            [
                velocity_table[member][first] * velocity_table[member][second]
                for member in range(19)
            ],
            nonequil,
        )
        factor = 1.0 if first == second else 2.0
        magnitude_square = magnitude_square + factor * component * component
    magnitude = jnp.sqrt(magnitude_square)
    relaxation = 0.5 * (
        relax_base
        + jnp.sqrt(
            relax_base * relax_base
            + 18.0 * math.sqrt(2.0) * smagorinsky * smagorinsky * magnitude / density
        )
    )
    force_share = 1.0 - 0.5 / relaxation
    outputs = []
    for member in range(19):
        along_force = signed_sum(velocity_table[member], forcing)
        source = (
            force_share
            * weight_table[member]
            * (3.0 * (along_force - force_along) + 9.0 * projections[member] * along_force)
        )
        collided = fields[member] - nonequil[member] / relaxation + source
        outputs.append(jnp.where(solid == 1, fields[opposite[member]], collided))
    return jnp.stack(outputs)


def linear_share(fraction, offset):
    return fraction if offset else 1.0 - fraction


def propagate(collided):
    plane_count = collided.shape[1]
    row_count = collided.shape[2]
    padded = extended(collided, (("stream", 1), ("trans", 2)), 1)
    moved = []
    for member in range(19):
        start_x = 1 - velocity_table[member][0]
        start_y = 1 - velocity_table[member][1]
        moved.append(padded[member, start_x : start_x + plane_count, start_y : start_y + row_count])
    rolled = []
    for member in range(19):
        depth_shift = velocity_table[member][2]
        rolled.append(
            jnp.roll(moved[member], depth_shift, axis=-1) if depth_shift != 0 else moved[member]
        )
    return jnp.stack(rolled)


def weight_tables(
    block_support, block_fraction, plane_count, row_count, depth_count, total_rows, own_rank
):
    depth_index = block_support % depth_count
    remainder = block_support // depth_count
    column = remainder % total_rows
    plane_index = remainder // total_rows
    pair_iota = jnp.arange(plane_count * row_count, dtype=jnp.int32)
    depth_iota = jnp.arange(depth_count, dtype=jnp.int32)
    pair_weight = jnp.zeros((block_support.shape[0], plane_count * row_count), jnp.float32)
    for shift_x in (0, 1):
        for shift_y in (0, 1):
            local_row = column + shift_y - own_rank * row_count
            valid = (local_row >= 0) & (local_row < row_count)
            pair_index = jnp.where(valid, (plane_index + shift_x) * row_count + local_row, -1)
            share = linear_share(block_fraction[0], shift_x) * linear_share(
                block_fraction[1], shift_y
            )
            pair_weight = pair_weight + jnp.where(
                pair_iota[None, :] == pair_index[:, None], share[:, None], 0.0
            )
    depth_weight = jnp.where(
        depth_iota[None, :] == depth_index[:, None], (1.0 - block_fraction[2])[:, None], 0.0
    ) + jnp.where(depth_iota[None, :] == depth_index[:, None] + 1, block_fraction[2][:, None], 0.0)
    return (pair_weight, depth_weight)


def per_device(populations, solid, support, fractions, target, area):
    plane_count = populations.shape[1]
    row_count = populations.shape[2]
    depth_count = populations.shape[3]
    own_markers = support.shape[0]
    groups = lax.axis_size("trans")
    own_rank = lax.axis_index("trans")
    total_rows = row_count * groups
    group_support, group_fraction, group_target, group_area = (
        lax.all_gather(support, "trans", axis=0, tiled=True),
        lax.all_gather(fractions, "trans", axis=1, tiled=True),
        lax.all_gather(target, "trans", axis=1, tiled=True),
        lax.all_gather(area, "trans", axis=0, tiled=True),
    )
    group_count = group_support.shape[0]
    block_size = math.gcd(group_count, 256)
    block_count = group_count // block_size
    support_blocks = group_support.reshape(block_count, block_size)
    fraction_blocks = jnp.moveaxis(group_fraction.reshape(3, block_count, block_size), 1, 0)
    fields = populations
    own_force = jnp.zeros((3, own_markers), jnp.float32)
    for repeat in range(STEPS):
        density, momenta = moments(fields)
        velocity_field = jnp.stack(
            [momenta[dimension] / density for dimension in range(3)]
        ).reshape(3, plane_count * row_count, depth_count)

        def interpolate(block):
            pair_weight, depth_weight = weight_tables(
                block[0], block[1], plane_count, row_count, depth_count, total_rows, own_rank
            )
            along_pairs = jnp.einsum(
                "mp,cpd->cmd", pair_weight, velocity_field, precision=lax.Precision.HIGHEST
            )
            return jnp.sum(along_pairs * depth_weight[None], axis=2)

        block_velocity = lax.map(interpolate, (support_blocks, fraction_blocks))
        partial_velocity = jnp.moveaxis(block_velocity, 0, 1).reshape(3, group_count)
        velocity = lax.psum(partial_velocity, "trans")
        group_force = group_area * (group_target - velocity)
        own_force = lax.dynamic_slice_in_dim(group_force, own_rank * own_markers, own_markers, 1)
        force_blocks = jnp.moveaxis(group_force.reshape(3, block_count, block_size), 1, 0)

        def spread(total, block):
            pair_weight, depth_weight = weight_tables(
                block[0], block[1], plane_count, row_count, depth_count, total_rows, own_rank
            )
            weighted = block[2][:, :, None] * depth_weight[None]
            added = jnp.einsum(
                "mp,cmd->cpd", pair_weight, weighted, precision=lax.Precision.HIGHEST
            )
            return (total + added, None)

        forcing, unused = lax.scan(
            spread,
            jnp.zeros((3, plane_count * row_count, depth_count), jnp.float32),
            (support_blocks, fraction_blocks, force_blocks),
        )
        forcing = forcing.reshape(3, plane_count, row_count, depth_count)
        collided = collide(fields, density, momenta, forcing, solid)
        fields = propagate(collided)
    return (fields, own_force)


def solution(mesh):
    placed = (
        P(None, "stream", "trans", None),
        P("stream", "trans", None),
        P(("stream", "trans")),
        P(None, ("stream", "trans")),
        P(None, ("stream", "trans")),
        P(("stream", "trans")),
    )
    return jax.shard_map(
        per_device,
        mesh=mesh,
        in_specs=placed,
        out_specs=(P(None, "stream", "trans", None), P(None, ("stream", "trans"))),
        check_vma=False,
    )
```

profile of v0, /device:TPU:57, one launch (start us, length us, event | category | flops | bytes accessed | tf_op | source)
XLA Modules:
  0.0 1061.2 jit_solution(16544112606314576096)
XLA Ops:
  0.6 0.9 divide_bitcast_fusion.5
  1.8 0.7 copy-done.3
  2.4 114.1 %all_gather.15 = f32[3,4096]{1,0:T(4,128)S(1)} all-gather(f32[3,128]{1,0:T(4,128)S(1)} %copy-done.3), channel_id=1, replica_groups=mesh['stream'=32,'trans'=32] {'trans'}, dimensions={1}, use_global_device_ids=true | all-gather | bytes 50688 | tf_op jit(solution)/shard_map/all_gather | solution.py:183
  116.6 0.7 copy-done.5
  117.2 97.1 %all-gather.1 = s32[32,1,128]{2,1,0:T(1,128)S(1)} all-gather(s32[1,1,128]{2,1,0:T(1,128)S(1)} %bitcast.1171), channel_id=1, replica_groups=mesh['stream'=32,'trans'=32] {'trans'}, dimensions={0}, use_global_device_ids=true | all-gather | bytes 16896 | tf_op jit(solution)/shard_map/all_gather | solution.py:182
  214.4 0.5 broadcast.4006
  214.9 0.7 reduce.5
  215.6 11.6 %while.54 = (s32[]{:T(128)}, f32[16,3,256]{2,1,0:T(4,128)S(1)}, s32[16,256]{1,0:T(8,128)S(1)}, s32[]{:T(128)}, f32[16,3,256]{2,1,0:T(4,128)S(1)}, /*index=5*/f32...) while((s32[]{:T(128)}, f32[16,3,256]{2,1,0:T(4,128)S(1)}, s32[16,256]{1,0:T(8,128)S(1)}, s32[]{:T(128)}, ...), condition=%wide.region_2.3_spmd, body=%wide.region_0.2_spmd.sunk | while | flops 19297284 | bytes 340121 | solution.py:209
  215.8 0.5 fusion.364
  216.5 0.5 fusion.364
  217.2 0.5 fusion.364
  218.0 0.5 fusion.364
  218.7 0.5 fusion.364
  219.4 0.5 fusion.364
  220.2 0.5 fusion.364
  220.9 0.5 fusion.364
  221.6 0.5 fusion.364
  222.3 0.5 fusion.364
  223.1 0.5 fusion.364
  223.8 0.5 fusion.364
  224.5 0.5 fusion.364
  225.2 0.5 fusion.364
  226.0 0.5 fusion.364
  226.7 0.5 fusion.364
  227.3 198.2 %psum.14 = f32[3,4096]{1,0:T(4,128)S(1)} all-reduce(f32[3,4096]{1,0:T(4,128)S(1)} %bitcast.1124), channel_id=1, replica_groups=mesh['stream'=32,'trans'=32] {'trans'}, use_global_device_ids=true, to_apply=%region_3.4 | all-reduce | flops 12288 | bytes 98304 | tf_op jit(solution)/shard_map/psum | solution.py:211
  425.5 98.1 %all_gather.13 = f32[3,4096]{1,0:T(4,128)S(1)} all-gather(f32[3,128]{1,0:T(4,128)S(1)} %copy-done.4), channel_id=1, replica_groups=mesh['stream'=32,'trans'=32] {'trans'}, dimensions={1}, use_global_device_ids=true | all-gather | bytes 50688 | tf_op jit(solution)/shard_map/all_gather | solution.py:184
  523.6 0.7 copy-done.6
  524.2 98.6 %all-gather = f32[32,1,128]{2,1,0:T(1,128)S(1)} all-gather(f32[1,1,128]{2,1,0:T(1,128)S(1)} %bitcast.1172), channel_id=1, replica_groups=mesh['stream'=32,'trans'=32] {'trans'}, dimensions={0}, use_global_device_ids=true | all-gather | bytes 16896 | tf_op jit(solution)/shard_map/all_gather | solution.py:185
  622.8 12.5 %while.56 = (s32[]{:T(128)}, f32[3,16,128]{2,1,0:T(8,128)S(1)}, f32[16,3,256]{2,1,0:T(4,128)S(1)}, s32[16,256]{1,0:T(8,128)S(1)}, f32[16,3,256]{2,1,0:T(4,128)S(...) while((s32[]{:T(128)}, f32[3,16,128]{2,1,0:T(8,128)S(1)}, f32[16,3,256]{2,1,0:T(4,128)S(1)}, ...), condition=%wide.region_5.6_spmd.clone, body=%wide.region_4.5_spmd.clone.sunk | while | flops 19212036 | bytes 362659 | solution.py:226
  623.2 0.4 fusion.370
  624.0 0.4 fusion.370
  636.0 95.6 %collective-permute-start = (f32[19,1,8,128]{3,2,1,0:T(8,128)S(1)}, f32[19,1,8,128]{3,2,1,0:T(8,128)S(1)}, u32[]{:S(2)}, u32[]{:S(2)}) collective-permute-start(f32[19,1,8,128]{3,2,1,0:T(8,128)S(1)} %get-tuple-element.707), channel_id=1, source_target_pairs={{0,32},{32,64},{64,96},{96,128},{128,160},{160,192},{192,224},{224... | collective-permute-start | bytes 233480 | tf_op jit(solution)/shard_map/ppermute | solution.py:44
  731.6 1.9 collective-permute-start.1
  733.7 14.5 %collective-permute-done.1 = f32[19,1,8,128]{3,2,1,0:T(8,128)S(1)} collective-permute-done((f32[19,1,8,128]{3,2,1,0:T(8,128)S(1)}, f32[19,1,8,128]{3,2,1,0:T(8,128)S(1)}, u32[]{:S(2)}, u32[]{:S(2)}) %collective-permute-start.1) | collective-permute-done | bytes 77856 | tf_op jit(solution)/shard_map/ppermute | solution.py:47
  748.2 1.9 collective-permute-start.2
  750.2 12.1 %collective-permute-start.3 = (f32[19,4,1,128]{3,2,1,0:T(1,128)S(1)}, f32[19,4,1,128]{3,2,1,0:T(1,128)S(1)}, u32[]{:S(2)}, u32[]{:S(2)}) collective-permute-start(f32[19,4,1,128]{3,2,1,0:T(1,128)S(1)} %get-tuple-element.694), channel_id=1, source_target_pairs={{1,0},{2,1},{3,2},{4,3},{5,4},{6,5},{7,6},{8,7},{9,8},{10,9},{11,1... | collective-permute-start | bytes 116744 | tf_op jit(solution)/shard_map/ppermute | solution.py:47
  762.5 0.8 collective-permute-done.3
  763.8 11.6 %while.55 = (s32[]{:T(128)}, f32[16,3,256]{2,1,0:T(4,128)S(1)}, s32[16,256]{1,0:T(8,128)S(1)}, s32[]{:T(128)}, f32[16,3,256]{2,1,0:T(4,128)S(1)}, /*index=5*/f32...) while((s32[]{:T(128)}, f32[16,3,256]{2,1,0:T(4,128)S(1)}, s32[16,256]{1,0:T(8,128)S(1)}, s32[]{:T(128)}, ...), condition=%wide.region_8.9_spmd, body=%wide.region_6.8_spmd.sunk | while | flops 19297284 | bytes 340121 | solution.py:209
  764.0 0.5 fusion.367
  764.7 0.5 fusion.367
  765.5 0.5 fusion.367
  766.2 0.5 fusion.367
  766.9 0.5 fusion.367
  767.6 0.5 fusion.367
  768.4 0.5 fusion.367
  769.1 0.5 fusion.367
  769.8 0.5 fusion.367
  770.5 0.5 fusion.367
  771.3 0.5 fusion.367
  772.0 0.5 fusion.367
  772.7 0.5 fusion.367
  773.5 0.5 fusion.367
  774.2 0.5 fusion.367
  774.9 0.5 fusion.367
  775.5 207.4 %psum.15 = f32[3,4096]{1,0:T(4,128)S(1)} all-reduce(f32[3,4096]{1,0:T(4,128)S(1)} %bitcast.1123), channel_id=1, replica_groups=mesh['stream'=32,'trans'=32] {'trans'}, use_global_device_ids=true, to_apply=%region_9.10 | all-reduce | flops 12288 | bytes 98304 | tf_op jit(solution)/shard_map/psum | solution.py:211
  982.9 12.5 %while.57 = (s32[]{:T(128)}, f32[3,16,128]{2,1,0:T(8,128)S(1)}, f32[16,3,256]{2,1,0:T(4,128)S(1)}, s32[16,256]{1,0:T(8,128)S(1)}, f32[16,3,256]{2,1,0:T(4,128)S(...) while((s32[]{:T(128)}, f32[3,16,128]{2,1,0:T(8,128)S(1)}, ...), condition=%wide.region_11.12_spmd.clone, body=%wide.region_10.11_spmd.clone.sunk | while | flops 19212036 | bytes 362659 | solution.py:226
  996.1 31.3 %collective-permute-start.4 = (f32[19,1,8,128]{3,2,1,0:T(8,128)S(1)}, f32[19,1,8,128]{3,2,1,0:T(8,128)S(1)}, u32[]{:S(2)}, u32[]{:S(2)}) collective-permute-start(f32[19,1,8,128]{3,2,1,0:T(8,128)S(1)} %get-tuple-element.704), channel_id=1, source_target_pairs={{0,32},{32,64},{64,96},{96,128},{128,160},{160,192},{192,224},{224... | collective-permute-start | bytes 233480 | tf_op jit(solution)/shard_map/ppermute | solution.py:44
  1027.4 1.9 collective-permute-start.5
  1029.5 0.6 constant_dynamic-slice_fusion.16
  1030.1 13.9 %collective-permute-done.5 = f32[19,1,8,128]{3,2,1,0:T(8,128)S(1)} collective-permute-done((f32[19,1,8,128]{3,2,1,0:T(8,128)S(1)}, f32[19,1,8,128]{3,2,1,0:T(8,128)S(1)}, u32[]{:S(2)}, u32[]{:S(2)}) %collective-permute-start.5) | collective-permute-done | bytes 77856 | tf_op jit(solution)/shard_map/ppermute | solution.py:47
  1044.0 1.9 collective-permute-start.6
  1045.9 12.1 %collective-permute-start.7 = (f32[19,4,1,128]{3,2,1,0:T(1,128)S(1)}, f32[19,4,1,128]{3,2,1,0:T(1,128)S(1)}, u32[]{:S(2)}, u32[]{:S(2)}) collective-permute-start(f32[19,4,1,128]{3,2,1,0:T(1,128)S(1)} %get-tuple-element.690), channel_id=1, source_target_pairs={{1,0},{2,1},{3,2},{4,3},{5,4},{6,5},{7,6},{8,7},{9,8},{10,9},{11,1... | collective-permute-start | bytes 116744 | tf_op jit(solution)/shard_map/ppermute | solution.py:47
  1058.1 1.0 collective-permute-done.7
  1060.5 0.7 copy-done.1
  (717 shorter events, 28.8 us)
Async XLA Ops:
  0.6 1.1 copy-start
  1.8 0.7 copy-start.3
  116.5 0.7 copy-start.5
  227.2 198.2 %copy-start.4 = (f32[3,128]{1,0:T(4,128)S(1)}, f32[3,128]{1,0:T(4,128)}, u32[]{:S(2)}) copy-start(f32[3,128]{1,0:T(4,128)} %param.18) | copy-start | bytes 4612
  523.6 0.7 copy-start.6
  622.8 12.5 %copy-start.2 = (s32[2,8,128]{2,1,0:T(8,128)S(1)}, s32[2,8,128]{2,1,0:T(8,128)}, u32[]{:S(2)}) copy-start(s32[2,8,128]{2,1,0:T(8,128)} %param.15) | copy-start | bytes 24580
  636.0 97.7 %collective-permute-start = (f32[19,1,8,128]{3,2,1,0:T(8,128)S(1)}, f32[19,1,8,128]{3,2,1,0:T(8,128)S(1)}, u32[]{:S(2)}, u32[]{:S(2)}) collective-permute-start(f32[19,1,8,128]{3,2,1,0:T(8,128)S(1)} %get-tuple-element.707), channel_id=1, source_target_pairs={{0,32},{32,64},{64,96},{96,128},{128,160},{160,192},{192,224},{224... | collective-permute-start | bytes 233480 | tf_op jit(solution)/shard_map/ppermute | solution.py:44
  731.6 16.6 %collective-permute-start.1 = (f32[19,1,8,128]{3,2,1,0:T(8,128)S(1)}, f32[19,1,8,128]{3,2,1,0:T(8,128)S(1)}, u32[]{:S(2)}, u32[]{:S(2)}) collective-permute-start(f32[19,1,8,128]{3,2,1,0:T(8,128)S(1)} %get-tuple-element.706), channel_id=1, source_target_pairs={{32,0},{64,32},{96,64},{128,96},{160,128},{192,160},{224,192},{256... | collective-permute-start | bytes 233480 | tf_op jit(solution)/shard_map/ppermute | solution.py:47
  748.2 14.2 %collective-permute-start.2 = (f32[19,4,1,128]{3,2,1,0:T(1,128)S(1)}, f32[19,4,1,128]{3,2,1,0:T(1,128)S(1)}, u32[]{:S(2)}, u32[]{:S(2)}) collective-permute-start(f32[19,4,1,128]{3,2,1,0:T(1,128)S(1)} %get-tuple-element.695), channel_id=1, source_target_pairs={{0,1},{1,2},{2,3},{3,4},{4,5},{5,6},{6,7},{7,8},{8,9},{9,10},{10,1... | collective-permute-start | bytes 116744 | tf_op jit(solution)/shard_map/ppermute | solution.py:44
  750.2 13.1 %collective-permute-start.3 = (f32[19,4,1,128]{3,2,1,0:T(1,128)S(1)}, f32[19,4,1,128]{3,2,1,0:T(1,128)S(1)}, u32[]{:S(2)}, u32[]{:S(2)}) collective-permute-start(f32[19,4,1,128]{3,2,1,0:T(1,128)S(1)} %get-tuple-element.694), channel_id=1, source_target_pairs={{1,0},{2,1},{3,2},{4,3},{5,4},{6,5},{7,6},{8,7},{9,8},{10,9},{11,1... | collective-permute-start | bytes 116744 | tf_op jit(solution)/shard_map/ppermute | solution.py:47
  996.1 34.0 %collective-permute-start.4 = (f32[19,1,8,128]{3,2,1,0:T(8,128)S(1)}, f32[19,1,8,128]{3,2,1,0:T(8,128)S(1)}, u32[]{:S(2)}, u32[]{:S(2)}) collective-permute-start(f32[19,1,8,128]{3,2,1,0:T(8,128)S(1)} %get-tuple-element.704), channel_id=1, source_target_pairs={{0,32},{32,64},{64,96},{96,128},{128,160},{160,192},{192,224},{224... | collective-permute-start | bytes 233480 | tf_op jit(solution)/shard_map/ppermute | solution.py:44
  1027.4 16.5 %collective-permute-start.5 = (f32[19,1,8,128]{3,2,1,0:T(8,128)S(1)}, f32[19,1,8,128]{3,2,1,0:T(8,128)S(1)}, u32[]{:S(2)}, u32[]{:S(2)}) collective-permute-start(f32[19,1,8,128]{3,2,1,0:T(8,128)S(1)} %get-tuple-element.703), channel_id=1, source_target_pairs={{32,0},{64,32},{96,64},{128,96},{160,128},{192,160},{224,192},{256... | collective-permute-start | bytes 233480 | tf_op jit(solution)/shard_map/ppermute | solution.py:47
  1044.0 14.0 %collective-permute-start.6 = (f32[19,4,1,128]{3,2,1,0:T(1,128)S(1)}, f32[19,4,1,128]{3,2,1,0:T(1,128)S(1)}, u32[]{:S(2)}, u32[]{:S(2)}) collective-permute-start(f32[19,4,1,128]{3,2,1,0:T(1,128)S(1)} %get-tuple-element.691), channel_id=1, source_target_pairs={{0,1},{1,2},{2,3},{3,4},{4,5},{5,6},{6,7},{7,8},{8,9},{9,10},{10,1... | collective-permute-start | bytes 116744 | tf_op jit(solution)/shard_map/ppermute | solution.py:44
  1045.9 13.1 %collective-permute-start.7 = (f32[19,4,1,128]{3,2,1,0:T(1,128)S(1)}, f32[19,4,1,128]{3,2,1,0:T(1,128)S(1)}, u32[]{:S(2)}, u32[]{:S(2)}) collective-permute-start(f32[19,4,1,128]{3,2,1,0:T(1,128)S(1)} %get-tuple-element.690), channel_id=1, source_target_pairs={{1,0},{2,1},{3,2},{4,3},{5,4},{6,5},{7,6},{8,7},{9,8},{10,9},{11,1... | collective-permute-start | bytes 116744 | tf_op jit(solution)/shard_map/ppermute | solution.py:47
  1060.5 0.7 copy-start.1
where the time goes:
time: 1060 us
  blocking collectives  814 us (77%)
  starting transfers between devices  159 us (15%)
  matrix products  30.2 us (3%)
  waiting for transfers between devices  30.2 us (3%)
  other arithmetic  14 us (1%)
    psum x2, blocking collectives, per_device(): velocity = lax.psum(partial_velocity, 'trans')  406 us
    ppermute x4, starting transfers between devices, extended(): lax.ppermute(lax.slice_in_dim(block, block.shape[dim] - width, None, axis...  131 us
    all_gather x1, blocking collectives, per_device(): lax.all_gather(fractions, 'trans', axis=1, tiled=True)  114 us
    all_gather x1, blocking collectives, per_device(): lax.all_gather(area, 'trans', axis=0, tiled=True)  98.6 us
    all_gather x1, blocking collectives, per_device(): lax.all_gather(target, 'trans', axis=1, tiled=True)  98.1 us
    all_gather x1, blocking collectives, per_device(): lax.all_gather(support, 'trans', axis=0, tiled=True)  97.1 us
    ppermute x4, waiting for transfers between devices, extended(): lax.ppermute(lax.slice_in_dim(block, 0, width, axis=dim), axis, backward)  30.2 us
    ppermute x4, starting transfers between devices, extended(): lax.ppermute(lax.slice_in_dim(block, 0, width, axis=dim), axis, backward)  28 us
  transfers between devices with their start and end apart: 8, of which 4 were waited for; matrix products, arithmetic and copies ran while one was open for 0% of the time, Pallas kernels for 0%

commit v1 on v0

v1 whole, which is shorter than its diff:
```python
import functools
import math

import jax
import jax.numpy as jnp
from jax import lax
from jax.experimental import pallas as pl
from jax.experimental.pallas import tpu as pltpu
from jax.sharding import PartitionSpec as P

STEPS = 2
VEL = (
    (0, 0, 0),
    (1, 0, 0),
    (-1, 0, 0),
    (0, 1, 0),
    (0, -1, 0),
    (0, 0, 1),
    (0, 0, -1),
    (1, 1, 0),
    (-1, -1, 0),
    (1, -1, 0),
    (-1, 1, 0),
    (1, 0, 1),
    (-1, 0, -1),
    (1, 0, -1),
    (-1, 0, 1),
    (0, 1, 1),
    (0, -1, -1),
    (0, 1, -1),
    (0, -1, 1),
)
WEIGHT = (1.0 / 3.0,) + (1.0 / 18.0,) * 6 + (1.0 / 36.0,) * 12
OPP = (0, 2, 1, 4, 3, 6, 5, 8, 7, 10, 9, 12, 11, 14, 13, 16, 15, 18, 17)
TAU_BASE = 0.8
SMAG = 0.17
MESH = pl.DeviceIdType.MESH
UP = 0
DOWN = 1
GO_RIGHT = (1, 7, 9, 11, 13)
GO_LEFT = (2, 8, 10, 12, 14)
ROWS_UP = ((3, 0, 0), (3, 1, 1), (15, 0, 0), (15, 1, 1), (17, 0, 0), (17, 1, 1), (7, 0, 1), (10, 1, 0))
ROWS_DOWN = ((4, 0, 0), (4, 1, 1), (16, 0, 0), (16, 1, 1), (18, 0, 0), (18, 1, 1), (8, 1, 0), (9, 0, 1))


def add_up(terms):
    total = None
    for sign, value in terms:
        if sign == 0:
            continue
        if total is None:
            total = value if sign > 0 else -value
        else:
            total = total + value if sign > 0 else total - value
    return total


def combine(factors, values):
    total = add_up(zip(factors, values))
    return 0.0 if total is None else total


def moments(f):
    rho = add_up((1, f[i]) for i in range(19))
    mom = [add_up((VEL[i][d], f[i]) for i in range(19)) for d in range(3)]
    return rho, mom


def collide(f, rho, mom, g, solid):
    inv_rho = 1.0 / rho
    u = [(mom[d] + 0.5 * g[d]) * inv_rho for d in range(3)]
    square = u[0] * u[0] + u[1] * u[1] + u[2] * u[2]
    ug = u[0] * g[0] + u[1] * g[1] + u[2] * g[2]
    base = 1.0 - 1.5 * square
    proj = [combine(VEL[i], u) for i in range(19)]
    neq = []
    for i in range(19):
        feq = WEIGHT[i] * rho * (base + 3.0 * proj[i] + 4.5 * proj[i] * proj[i])
        neq.append(f[i] - feq)
    mag2 = 0.0
    for a, b in ((0, 0), (1, 1), (2, 2), (0, 1), (0, 2), (1, 2)):
        comp = combine([VEL[i][a] * VEL[i][b] for i in range(19)], neq)
        mag2 = mag2 + (1.0 if a == b else 2.0) * comp * comp
    mag = jnp.sqrt(mag2)
    tau = 0.5 * (
        TAU_BASE + jnp.sqrt(TAU_BASE * TAU_BASE + 18.0 * math.sqrt(2.0) * SMAG * SMAG * mag * inv_rho)
    )
    inv_tau = 1.0 / tau
    share = 1.0 - 0.5 * inv_tau
    is_solid = solid == 1
    out = []
    for i in range(19):
        cg = combine(VEL[i], g)
        source = share * (WEIGHT[i] * (3.0 * (cg - ug) + 9.0 * proj[i] * cg))
        out.append(jnp.where(is_solid, f[OPP[i]], f[i] - neq[i] * inv_tau + source))
    return out


def split(x):
    hi = x.astype(jnp.bfloat16)
    lo = (x - hi.astype(jnp.float32)).astype(jnp.bfloat16)
    return jnp.concatenate([hi, lo], axis=0)


def kernel(
    n_stream,
    n_trans,
    per_chunk,
    pop_ref,
    solid_ref,
    support_ref,
    frac_ref,
    target_ref,
    area_ref,
    out_ref,
    force_ref,
    gath,
    onehot,
    vs,
    gsum,
    htile,
    hrecv,
    hbuf,
    xsend,
    xrecv,
    ysend,
    yrecv,
    msend,
    mrecv,
    mown,
    dsend,
    drecv,
    uret,
    urecv,
    g_send,
    g_recv,
    h_send,
    h_recv,
    x_send,
    x_recv,
    y_send,
    y_recv,
    m_send,
    m_recv,
    d_send,
    d_recv,
    u_send,
    u_recv,
):
    s = lax.axis_index("stream")
    t = lax.axis_index("trans")
    s_next = lax.rem(s + 1, n_stream)
    s_prev = lax.rem(s + n_stream - 1, n_stream)
    t_next = lax.rem(t + 1, n_trans)
    t_prev = lax.rem(t + n_trans - 1, n_trans)
    diagonals = ((s_next, t_next), (s_prev, t_next), (s_next, t_prev), (s_prev, t_prev))

    barrier = pltpu.get_barrier_semaphore()

    def greet(k, carry):
        pl.semaphore_signal(
            barrier, inc=1, device_id=(s, lax.rem(t + k, n_trans)), device_id_type=MESH
        )
        return carry

    lax.fori_loop(1, n_trans, greet, 0)
    for where in ((s_next, t), (s_prev, t)) + diagonals:
        pl.semaphore_signal(barrier, inc=1, device_id=where, device_id_type=MESH)

    gath[0, 0:1, :] = support_ref[...].astype(jnp.float32)
    gath[0, 1:4, :] = frac_ref[...]
    gath[0, 4:7, :] = target_ref[...]
    gath[0, 7:8, :] = area_ref[...]

    f = [pop_ref[i] for i in range(19)]
    rho, mom = moments(f)
    inv = 1.0 / rho
    ustar = [mom[d] * inv for d in range(3)]
    htile[...] = jnp.zeros_like(htile)
    for p in range(2):
        for d in range(3):
            htile[UP, p * 4 + d : p * 4 + d + 1, :] = ustar[d][p, 7:8, :]
            htile[DOWN, p * 4 + d : p * 4 + d + 1, :] = ustar[d][p, 0:1, :]

    pl.semaphore_wait(barrier, n_trans - 1 + 6)

    def remote(src, dst, send, recv, where):
        return pltpu.make_async_remote_copy(
            src_ref=src, dst_ref=dst, send_sem=send, recv_sem=recv, device_id=where, device_id_type=MESH
        )

    copies = []

    def launch(*args):
        copy = remote(*args)
        copy.start()
        copies.append(copy)
        return copy

    halo = [
        launch(htile.at[UP], hrecv.at[UP], h_send.at[UP], h_recv.at[UP], (s, t_next)),
        launch(htile.at[DOWN], hrecv.at[DOWN], h_send.at[DOWN], h_recv.at[DOWN], (s, t_prev)),
    ]

    def gather_copy(k):
        return remote(
            gath.at[0], gath.at[k], g_send.at[k], g_recv.at[k], (s, lax.rem(t + k, n_trans))
        )

    def start_gather(k, carry):
        gather_copy(k).start()
        return carry

    lax.fori_loop(1, n_trans, start_gather, 0)

    for copy in halo:
        copy.wait_recv()

    hbuf[...] = jnp.zeros_like(hbuf)

    def set_halo(lo, hi):
        for p in range(2):
            hbuf[p, 0:3, :] = lo[p * 4 : p * 4 + 3, :]
            hbuf[p, 3:6, :] = hi[p * 4 : p * 4 + 3, :]

    def set_velocity(ustar):
        rows = []
        for shift in (0, 1):
            for d in range(3):
                for p in range(2):
                    x = ustar[d][p]
                    rows.append(pltpu.roll(x, 127, 1) if shift else x)
        for shift in (0, 1):
            for p in range(2):
                x = hbuf[p]
                rows.append(pltpu.roll(x, 127, 1) if shift else x)
        vs[...] = split(jnp.concatenate(rows, axis=0))

    set_halo(hrecv[UP], hrecv[DOWN])
    set_velocity(ustar)

    width = per_chunk * 128
    first_row = (t * 8).astype(jnp.float32)

    def marker_pass(step):
        gsum[...] = jnp.zeros_like(gsum)

        def chunk(j, carry):
            tile = jnp.concatenate([gath[j * per_chunk + i] for i in range(per_chunk)], axis=1)
            fx, fy, fz = tile[1:2], tile[2:3], tile[3:4]
            b = jnp.floor(tile[0:1] * (1.0 / 128.0))
            if step == 0:
                e = tile[0:1] - 128.0 * b
                depth = lax.broadcasted_iota(jnp.int32, (128, width), 0).astype(jnp.float32)
                pick = jnp.where(depth == e, 1.0, 0.0).astype(jnp.bfloat16)
                onehot[j] = pick
            else:
                pick = onehot[j]
            r = lax.dot_general(
                vs[...], pick, (((1,), (0,)), ((), ())), preferred_element_type=jnp.float32
            )
            r = r[0:128] + r[128:256]
            gx, gy, gz = 1.0 - fx, 1.0 - fy, 1.0 - fz
            local = lax.broadcasted_iota(jnp.int32, (8, width), 0).astype(jnp.float32)
            rel = b - first_row
            wy = jnp.where(local == rel, gy, 0.0) + jnp.where(local == rel + 1.0, fy, 0.0)
            wh = jnp.where(
                local < 3.0, jnp.where(rel == -1.0, gy, 0.0), jnp.where(rel == 7.0, fy, 0.0)
            )

            def lerp(at):
                planes = []
                for p in range(2):
                    low, high = at(0, p), at(1, p)
                    planes.append(low * gz + high * fz)
                return planes[0] * gx + planes[1] * fx

            edge = wh * lerp(lambda shift, p: r[(12 + shift * 2 + p) * 8 : (12 + shift * 2 + p) * 8 + 8])
            vel = []
            for d in range(3):
                own = lerp(
                    lambda shift, p: r[((shift * 3 + d) * 2 + p) * 8 : ((shift * 3 + d) * 2 + p) * 8 + 8]
                )
                vel.append(
                    jnp.sum(wy * own, axis=0, keepdims=True) + edge[d : d + 1] + edge[3 + d : 4 + d]
                )
            if step == STEPS - 1:
                mine = (rel >= 0.0) & (rel <= 7.0)
                for d in range(3):
                    back = jnp.where(mine, vel[d], 0.0)
                    for i in range(per_chunk):
                        uret[j * per_chunk + i, d : d + 1, :] = back[:, i * 128 : i * 128 + 128]
            spread = []
            wyz = [wy * gz, wy * fz]
            wx = (gx, fx)
            pushes = [tile[7:8] * (tile[4 + d : 5 + d] - vel[d]) for d in range(3)]
            for shift in (0, 1):
                for d in range(3):
                    for p in range(2):
                        spread.append(wyz[shift] * (pushes[d] * wx[p]))
            gsum[...] += lax.dot_general(
                split(jnp.concatenate(spread, axis=0)),
                pick,
                (((1,), (1,)), ((), ())),
                preferred_element_type=jnp.float32,
            )
            return carry

        lax.fori_loop(0, n_trans // per_chunk, chunk, 0)
        total = gsum[0:96] + gsum[96:192]
        g = []
        for d in range(3):
            planes = []
            for p in range(2):
                low = total[(d * 2 + p) * 8 : (d * 2 + p) * 8 + 8]
                high = total[((3 + d) * 2 + p) * 8 : ((3 + d) * 2 + p) * 8 + 8]
                planes.append(low + pltpu.roll(high, 1, 1))
            g.append(jnp.stack(planes))
        return g

    def wait_gather(k, carry):
        gather_copy(k).wait_recv()
        return carry

    lax.fori_loop(1, n_trans, wait_gather, 0)

    row_of = lax.broadcasted_iota(jnp.int32, (8, 128), 0)

    def deep(post):
        return [
            [
                pltpu.roll(post[i][p], VEL[i][2] % 128, 1) if VEL[i][2] else post[i][p]
                for p in range(2)
            ]
            for i in range(19)
        ]

    def exchange(step, moved):
        sent = []
        for q, i in enumerate(GO_RIGHT):
            xsend[step, 0, q] = moved[i][1]
        for q, i in enumerate(GO_LEFT):
            xsend[step, 1, q] = moved[i][0]
        sent.append(launch(xsend.at[step, 0], xrecv.at[step, 0], x_send.at[step, 0], x_recv.at[step, 0], (s_next, t)))
        sent.append(launch(xsend.at[step, 1], xrecv.at[step, 1], x_send.at[step, 1], x_recv.at[step, 1], (s_prev, t)))
        for q, (i, source, unused) in enumerate(ROWS_UP):
            ysend[step, UP, q : q + 1, :] = moved[i][source][7:8]
        for q, (i, source, unused) in enumerate(ROWS_DOWN):
            ysend[step, DOWN, q : q + 1, :] = moved[i][source][0:1]
        sent.append(launch(ysend.at[step, UP], yrecv.at[step, UP], y_send.at[step, UP], y_recv.at[step, UP], (s, t_next)))
        sent.append(launch(ysend.at[step, DOWN], yrecv.at[step, DOWN], y_send.at[step, DOWN], y_recv.at[step, DOWN], (s, t_prev)))
        corner = ((7, 1, 7), (10, 0, 7), (9, 1, 0), (8, 0, 0))
        for q, (i, source, row) in enumerate(corner):
            dsend[step, q] = jnp.broadcast_to(moved[i][source][row : row + 1], (8, 128))
        if step < STEPS - 1:
            for side, sign, row in ((UP, 1, 7), (DOWN, -1, 0)):
                inner = row - sign
                for p in range(2):
                    level = {0: [], sign: []}
                    own = []
                    for i in range(19):
                        source = p - VEL[i][0]
                        if source not in (0, 1):
                            continue
                        if VEL[i][1] in level:
                            level[VEL[i][1]].append((i, moved[i][source]))
                        else:
                            own.append((i, moved[i][source]))
                    for m in range(4):
                        flat = sum_moment(level[0], m)
                        steep = sum_moment(level[sign], m)
                        value = 0.0
                        if flat is not None:
                            value = flat[row : row + 1]
                        if steep is not None:
                            value = value + steep[inner : inner + 1]
                        msend[side, p * 4 + m : p * 4 + m + 1, :] = value
                        mine = sum_moment(own, m)
                        mown[side, p * 4 + m : p * 4 + m + 1, :] = (
                            jnp.zeros((1, 128), jnp.float32) if mine is None else mine[7 - row : 8 - row]
                        )
                for q, names, source, at in ((0, GO_RIGHT, 1, 0), (1, GO_LEFT, 0, 4)):
                    q = q + (0 if side == UP else 2)
                    flat_set = [(i, moved[i][source]) for i in names if VEL[i][1] == 0]
                    steep_set = [(i, moved[i][source]) for i in names if VEL[i][1] == sign]
                    for m in range(4):
                        flat = sum_moment(flat_set, m)
                        steep = sum_moment(steep_set, m)
                        value = 0.0
                        if flat is not None:
                            value = flat[row : row + 1]
                        if steep is not None:
                            value = value + steep[inner : inner + 1]
                        dsend[step, q, at + m : at + m + 1, :] = value
            sent.append(launch(msend.at[UP], mrecv.at[UP], m_send.at[UP], m_recv.at[UP], (s, t_next)))
            sent.append(launch(msend.at[DOWN], mrecv.at[DOWN], m_send.at[DOWN], m_recv.at[DOWN], (s, t_prev)))
        for q, where in enumerate(diagonals):
            sent.append(launch(dsend.at[step, q], drecv.at[step, q], d_send.at[step, q], d_recv.at[step, q], where))
        return sent

    def sum_moment(members, m):
        if m == 0:
            return add_up((1, value) for i, value in members)
        return add_up((VEL[i][m - 1], value) for i, value in members)

    def stream(step, moved):
        new = []
        for i in range(19):
            cx, cy, unused = VEL[i]
            planes = []
            for p in range(2):
                source = p - cx
                if source in (0, 1):
                    tile = moved[i][source]
                elif cx == 1:
                    tile = xrecv[step, 0, GO_RIGHT.index(i)]
                else:
                    tile = xrecv[step, 1, GO_LEFT.index(i)]
                if cy != 0:
                    side = UP if cy == 1 else DOWN
                    rows = ROWS_UP if cy == 1 else ROWS_DOWN
                    if source in (0, 1):
                        at = rows.index((i, source, p))
                        edge = yrecv[step, side, at : at + 1, :]
                    else:
                        q = (0 if cx == 1 else 1) + (0 if cy == 1 else 2)
                        at = 4 if cx == 1 else 0
                        edge = drecv[step, q, at : at + 1, :]
                    tile = jnp.where(row_of == (0 if cy == 1 else 7), edge, pltpu.roll(tile, cy % 8, 0))
                planes.append(tile)
            new.append(jnp.stack(planes))
        return new

    def edge_moments(step, side):
        low = row_of < 4
        total = mrecv[side] + mown[side]
        q = 0 if side == UP else 2
        total = total + jnp.where(low, drecv[step, q], drecv[step, q + 1])
        sign = 1 if side == UP else -1
        row = 0 if side == UP else 7
        i = 9 if side == UP else 7
        left = xrecv[step, 0, GO_RIGHT.index(i), row : row + 1, :]
        i = 8 if side == UP else 10
        right = xrecv[step, 1, GO_LEFT.index(i), row : row + 1, :]
        total = total + jnp.where((row_of == 0) | (row_of == 1), left, 0.0)
        total = total + jnp.where(row_of == 2, -sign * left, 0.0)
        total = total + jnp.where(row_of == 4, right, 0.0)
        total = total + jnp.where(row_of == 5, -right, 0.0)
        total = total + jnp.where(row_of == 6, -sign * right, 0.0)
        return total

    def edge_velocity(total):
        values = []
        for p in range(2):
            inv = 1.0 / total[p * 4 : p * 4 + 1]
            values.append(total[p * 4 + 1 : p * 4 + 4] * inv)
        return values

    solid = solid_ref[...]

    g = marker_pass(0)
    moved = deep(collide(f, rho, mom, g, solid))
    for copy in exchange(0, moved):
        copy.wait_recv()
    f = stream(0, moved)
    low = edge_velocity(edge_moments(0, UP))
    high = edge_velocity(edge_moments(0, DOWN))
    for p in range(2):
        hbuf[p, 0:3, :] = low[p]
        hbuf[p, 3:6, :] = high[p]
    rho, mom = moments(f)
    inv = 1.0 / rho
    set_velocity([mom[d] * inv for d in range(3)])

    g = marker_pass(1)

    def return_copy(k):
        return remote(
            uret.at[k],
            urecv.at[k],
            u_send.at[k],
            u_recv.at[k],
            (s, lax.rem(t + n_trans - k, n_trans)),
        )

    def start_return(k, carry):
        return_copy(k).start()
        return carry

    lax.fori_loop(1, n_trans, start_return, 0)
    moved = deep(collide(f, rho, mom, g, solid))
    for copy in exchange(1, moved):
        copy.wait_recv()
    f = stream(1, moved)
    for i in range(19):
        out_ref[i] = f[i]

    def wait_return(k, carry):
        return_copy(k).wait_recv()
        return carry

    lax.fori_loop(1, n_trans, wait_return, 0)
    vel = uret[0]
    for k in range(1, n_trans):
        vel = vel + urecv[k]
    force_ref[...] = gath[0, 7:8, :] * (gath[0, 4:7, :] - vel[0:3])

    for copy in copies:
        copy.wait_send()

    def wait_sends(k, carry):
        gather_copy(k).wait_send()
        return_copy(k).wait_send()
        return carry

    lax.fori_loop(1, n_trans, wait_sends, 0)


def per_device(n_stream, n_trans, populations, solid, support, fractions, target, area):
    per_chunk = math.gcd(n_trans, 8)
    dma = pltpu.SemaphoreType.DMA
    f32 = jnp.float32
    vmem = pl.BlockSpec(memory_space=pltpu.VMEM)
    markers = support.shape[0]
    return pl.pallas_call(
        functools.partial(kernel, n_stream, n_trans, per_chunk),
        out_shape=(
            jax.ShapeDtypeStruct(populations.shape, f32),
            jax.ShapeDtypeStruct((3, markers), f32),
        ),
        in_specs=[vmem] * 6,
        out_specs=(vmem, vmem),
        scratch_shapes=[
            pltpu.VMEM((n_trans, 8, 128), f32),
            pltpu.VMEM((n_trans // per_chunk, 128, per_chunk * 128), jnp.bfloat16),
            pltpu.VMEM((256, 128), jnp.bfloat16),
            pltpu.VMEM((192, 128), f32),
            pltpu.VMEM((2, 8, 128), f32),
            pltpu.VMEM((2, 8, 128), f32),
            pltpu.VMEM((2, 8, 128), f32),
            pltpu.VMEM((2, 2, 5, 8, 128), f32),
            pltpu.VMEM((2, 2, 5, 8, 128), f32),
            pltpu.VMEM((2, 2, 8, 128), f32),
            pltpu.VMEM((2, 2, 8, 128), f32),
            pltpu.VMEM((2, 8, 128), f32),
            pltpu.VMEM((2, 8, 128), f32),
            pltpu.VMEM((2, 8, 128), f32),
            pltpu.VMEM((2, 4, 8, 128), f32),
            pltpu.VMEM((2, 4, 8, 128), f32),
            pltpu.VMEM((n_trans, 3, 128), f32),
            pltpu.VMEM((n_trans, 3, 128), f32),
            dma((n_trans,)),
            dma((n_trans,)),
            dma((2,)),
            dma((2,)),
            dma((2, 2)),
            dma((2, 2)),
            dma((2, 2)),
            dma((2, 2)),
            dma((2,)),
            dma((2,)),
            dma((2, 4)),
            dma((2, 4)),
            dma((n_trans,)),
            dma((n_trans,)),
        ],
        compiler_params=pltpu.CompilerParams(
            collective_id=0, has_side_effects=True, vmem_limit_bytes=40 * 1024 * 1024
        ),
        name="tract",
    )(
        populations,
        solid,
        support.reshape(1, markers),
        fractions,
        target,
        area.reshape(1, markers),
    )


def solution(mesh):
    placed = (
        P(None, "stream", "trans", None),
        P("stream", "trans", None),
        P(("stream", "trans")),
        P(None, ("stream", "trans")),
        P(None, ("stream", "trans")),
        P(("stream", "trans")),
    )
    return jax.shard_map(
        functools.partial(per_device, mesh.shape["stream"], mesh.shape["trans"]),
        mesh=mesh,
        in_specs=placed,
        out_specs=(P(None, "stream", "trans", None), P(None, ("stream", "trans"))),
        check_vma=False,
    )
```

time: 1060 us -> 61.5 us (0.06)
  the two profiles are of different devices: /device:TPU:57 before, /device:TPU:1 now
where the time goes in v1:
time: 61.5 us; the launch traced here: 61.2 us
  Pallas kernels  56.4 us (92%)
  local copies, waits for them, and re-layouts  4.2 us (7%)
  between operations  0.67 us (1%)
    pallas_call x1, Pallas kernels, per_device(): pl.pallas_call(functools.partial(kernel, n_stream, n_trans, per_chunk), o...  56.4 us
    unnamed x14, local copies, waits for them, and re-layouts  4.2 us

profile of v1, /device:TPU:1, one launch (start us, length us, event | category | flops | bytes accessed | tf_op | source)
XLA Modules:
  0.0 61.2 jit_solution(8569007087423353276)
XLA Ops:
  0.6 0.0 copy-start.2
  0.6 0.0 copy-start.4
  0.7 0.0 copy-start.5
  0.7 0.7 %copy-done.2 = f32[3,128]{1,0:T(4,128)S(1)} copy-done((f32[3,128]{1,0:T(4,128)S(1)}, f32[3,128]{1,0:T(4,128)}, u32[]{:S(2)}) %copy-start.2) | copy-done | bytes 1560
  1.3 0.0 copy-done.4
  1.3 0.0 copy-done.5
  1.3 0.0 copy-start
  1.3 0.9 %copy-done = f32[19,2,8,128]{3,2,1,0:T(8,128)S(1)} copy-done((f32[19,2,8,128]{3,2,1,0:T(8,128)S(1)}, f32[19,2,8,128]{3,2,1,0:T(8,128)}, u32[]{:S(2)}) %copy-start) | copy-done | bytes 155672
  2.2 0.0 copy-start.1
  2.2 0.7 %copy-done.1 = s32[2,8,128]{2,1,0:T(8,128)S(1)} copy-done((s32[2,8,128]{2,1,0:T(8,128)S(1)}, s32[2,8,128]{2,1,0:T(8,128)}, u32[]{:S(2)}) %copy-start.1) | copy-done | bytes 8216
  2.9 0.0 copy-start.3
  2.9 0.7 %copy-done.3 = f32[3,128]{1,0:T(4,128)S(1)} copy-done((f32[3,128]{1,0:T(4,128)S(1)}, f32[3,128]{1,0:T(4,128)}, u32[]{:S(2)}) %copy-start.3) | copy-done | bytes 1560
  3.6 56.4 %tract.1 = (f32[19,2,8,128]{3,2,1,0:T(8,128)S(1)}, f32[3,128]{1,0:T(4,128)S(1)}) custom-call(f32[19,2,8,128]{3,2,1,0:T(8,128)S(1)} %copy-done, s32[2,8,128]{2,1,0:T(8,128)S(1)} %copy-done.1, s32[1,128]{1,0:T(1,128)S(1)} %bitcast.2, f32[3,128]{1,0:T(4,128)S(1)} %copy-done.2, f32[3,128]{1,0:T(4,128)S(1)} %copy-done.3, f32[1,128]{1,0:T(1,128)S(1)} %bitcast.3), custom_call_target="tpu_custom_call" | custom-call | tf_op jit(solution)/shard_map/tract/pallas_call | solution.py:525
  60.0 0.7 %copy.10 = f32[19,2,8,128]{3,2,1,0:T(8,128)} copy(f32[19,2,8,128]{3,2,1,0:T(8,128)S(1)} %get-tuple-element.4) | data formatting | bytes 311296
  60.7 0.6 copy.11
Async XLA Ops:
  0.6 0.7 %copy-start.2 = (f32[3,128]{1,0:T(4,128)S(1)}, f32[3,128]{1,0:T(4,128)}, u32[]{:S(2)}) copy-start(f32[3,128]{1,0:T(4,128)} %frac_ref.1) | copy-start | bytes 4612
  0.6 0.7 %copy-start.4 = (s32[128]{0:T(128)S(1)}, s32[128]{0:T(128)}, u32[]{:S(2)}) copy-start(s32[128]{0:T(128)} %param.8) | copy-start | bytes 1540
  0.7 0.7 %copy-start.5 = (f32[128]{0:T(128)S(1)}, f32[128]{0:T(128)}, u32[]{:S(2)}) copy-start(f32[128]{0:T(128)} %param.11) | copy-start | bytes 1540
  1.3 0.9 %copy-start = (f32[19,2,8,128]{3,2,1,0:T(8,128)S(1)}, f32[19,2,8,128]{3,2,1,0:T(8,128)}, u32[]{:S(2)}) copy-start(f32[19,2,8,128]{3,2,1,0:T(8,128)} %pop_ref.1) | copy-start | bytes 466948
  2.2 0.7 %copy-start.1 = (s32[2,8,128]{2,1,0:T(8,128)S(1)}, s32[2,8,128]{2,1,0:T(8,128)}, u32[]{:S(2)}) copy-start(s32[2,8,128]{2,1,0:T(8,128)} %solid_ref.1) | copy-start | bytes 24580
  2.9 0.7 %copy-start.3 = (f32[3,128]{1,0:T(4,128)S(1)}, f32[3,128]{1,0:T(4,128)}, u32[]{:S(2)}) copy-start(f32[3,128]{1,0:T(4,128)} %target_ref.1) | copy-start | bytes 4612

commit v2 on v1

--- a/solution.py
+++ b/solution.py
@@ -96,28 +96,33 @@
     return out
 
 
-def split(x):
+def split(x, axis):
     hi = x.astype(jnp.bfloat16)
     lo = (x - hi.astype(jnp.float32)).astype(jnp.bfloat16)
-    return jnp.concatenate([hi, lo], axis=0)
+    return jnp.concatenate([hi, lo], axis=axis)
 
 
 def kernel(
     n_stream,
     n_trans,
-    per_chunk,
+    columns,
+    pop_hbm,
+    solid_hbm,
+    support_hbm,
+    frac_hbm,
+    target_hbm,
+    area_hbm,
+    out_ref,
+    force_ref,
     pop_ref,
     solid_ref,
     support_ref,
     frac_ref,
     target_ref,
     area_ref,
-    out_ref,
-    force_ref,
     gath,
     onehot,
     vs,
-    gsum,
     htile,
     hrecv,
     hbuf,
@@ -125,13 +130,14 @@
     xrecv,
     ysend,
     yrecv,
-    msend,
-    mrecv,
+    ylast,
+    ylast_recv,
     mown,
     dsend,
     drecv,
     uret,
     urecv,
+    in_sem,
     g_send,
     g_recv,
     h_send,
@@ -140,8 +146,6 @@
     x_recv,
     y_send,
     y_recv,
-    m_send,
-    m_recv,
     d_send,
     d_recv,
     u_send,
@@ -155,22 +159,50 @@
     t_prev = lax.rem(t + n_trans - 1, n_trans)
     diagonals = ((s_next, t_next), (s_prev, t_next), (s_next, t_prev), (s_prev, t_prev))
 
+    run = n_trans // columns
+    x = t // run
+    z = lax.rem(t, run)
+    upper = (2 * z) // run
+    far_first = [upper * q + (1 - upper) * (run - 1 - q) for q in range(run)]
+    far_columns = (2, 1, 3) if columns == 4 else tuple(range(1, columns))
+
+    def column(offset):
+        return lax.rem(x + offset, columns)
+
+    loads = [
+        pltpu.make_async_copy(source, target, in_sem.at[k])
+        for k, (source, target) in enumerate(
+            (
+                (pop_hbm, pop_ref),
+                (support_hbm, support_ref),
+                (frac_hbm, frac_ref),
+                (target_hbm, target_ref),
+                (area_hbm, area_ref),
+                (solid_hbm, solid_ref),
+            )
+        )
+    ]
     barrier = pltpu.get_barrier_semaphore()
 
-    def greet(k, carry):
-        pl.semaphore_signal(
-            barrier, inc=1, device_id=(s, lax.rem(t + k, n_trans)), device_id_type=MESH
-        )
-        return carry
-
-    lax.fori_loop(1, n_trans, greet, 0)
-    for where in ((s_next, t), (s_prev, t)) + diagonals:
+    def greet(where):
         pl.semaphore_signal(barrier, inc=1, device_id=where, device_id_type=MESH)
 
-    gath[0, 0:1, :] = support_ref[...].astype(jnp.float32)
-    gath[0, 1:4, :] = frac_ref[...]
-    gath[0, 4:7, :] = target_ref[...]
-    gath[0, 7:8, :] = area_ref[...]
+    for where in diagonals + ((s_next, t), (s_prev, t)):
+        greet(where)
+    for offset in far_columns:
+        for row in far_first:
+            greet((s, column(offset) * run + row))
+    for row in far_first:
+        pl.when(row != z)(functools.partial(greet, (s, x * run + row)))
+    for load in loads:
+        load.start()
+    for load in loads:
+        load.wait()
+
+    gath[t, 0:1, :] = support_ref[...].astype(jnp.float32)
+    gath[t, 1:4, :] = frac_ref[...]
+    gath[t, 4:7, :] = target_ref[...]
+    gath[t, 7:8, :] = area_ref[...]
 
     f = [pop_ref[i] for i in range(19)]
     rho, mom = moments(f)
@@ -203,15 +235,16 @@
     ]
 
     def gather_copy(k):
-        return remote(
-            gath.at[0], gath.at[k], g_send.at[k], g_recv.at[k], (s, lax.rem(t + k, n_trans))
-        )
-
-    def start_gather(k, carry):
-        gather_copy(k).start()
-        return carry
-
-    lax.fori_loop(1, n_trans, start_gather, 0)
+        return remote(gath.at[t], gath.at[t], g_send.at[k], g_recv.at[t], (s, k))
+
+    def gather_wait(k):
+        remote(gath.at[t], gath.at[k], g_send.at[k], g_recv.at[k], (s, k)).wait_recv()
+
+    for offset in far_columns:
+        for row in far_first:
+            gather_copy(column(offset) * run + row).start()
+    for row in far_first:
+        pl.when(row != z)(lambda row=row: gather_copy(x * run + row).start())
 
     for copy in halo:
         copy.wait_recv()
@@ -234,19 +267,30 @@
             for p in range(2):
                 x = hbuf[p]
                 rows.append(pltpu.roll(x, 127, 1) if shift else x)
-        vs[...] = split(jnp.concatenate(rows, axis=0))
+        vs[...] = split(jnp.concatenate(rows, axis=0), 1)
 
     set_halo(hrecv[UP], hrecv[DOWN])
     set_velocity(ustar)
 
-    width = per_chunk * 128
+    width = run * 128
     first_row = (t * 8).astype(jnp.float32)
 
+    def return_copy(k):
+        return remote(uret.at[k], urecv.at[t], u_send.at[k], u_recv.at[t], (s, k))
+
+    def return_wait(k):
+        remote(uret.at[k], urecv.at[k], u_send.at[k], u_recv.at[k], (s, k)).wait_recv()
+
     def marker_pass(step):
-        gsum[...] = jnp.zeros_like(gsum)
-
-        def chunk(j, carry):
-            tile = jnp.concatenate([gath[j * per_chunk + i] for i in range(per_chunk)], axis=1)
+        def chunk(j):
+            first = column(j) * run
+            if step == 0:
+                for i in range(run):
+                    if j:
+                        gather_wait(first + i)
+                    else:
+                        pl.when(z != i)(functools.partial(gather_wait, first + i))
+            tile = jnp.concatenate([gath[first + i] for i in range(run)], axis=1)
             fx, fy, fz = tile[1:2], tile[2:3], tile[3:4]
             b = jnp.floor(tile[0:1] * (1.0 / 128.0))
             if step == 0:
@@ -257,9 +301,11 @@
             else:
                 pick = onehot[j]
             r = lax.dot_general(
-                vs[...], pick, (((1,), (0,)), ((), ())), preferred_element_type=jnp.float32
+                vs[...],
+                jnp.concatenate([pick, pick], axis=0),
+                (((1,), (0,)), ((), ())),
+                preferred_element_type=jnp.float32,
             )
-            r = r[0:128] + r[128:256]
             gx, gy, gz = 1.0 - fx, 1.0 - fy, 1.0 - fz
             local = lax.broadcasted_iota(jnp.int32, (8, width), 0).astype(jnp.float32)
             rel = b - first_row
@@ -288,8 +334,13 @@
                 mine = (rel >= 0.0) & (rel <= 7.0)
                 for d in range(3):
                     back = jnp.where(mine, vel[d], 0.0)
-                    for i in range(per_chunk):
-                        uret[j * per_chunk + i, d : d + 1, :] = back[:, i * 128 : i * 128 + 128]
+                    for i in range(run):
+                        uret[first + i, d : d + 1, :] = back[:, i * 128 : i * 128 + 128]
+                for i in range(run):
+                    if j:
+                        return_copy(first + i).start()
+                    else:
+                        pl.when(z != i)(lambda i=i: return_copy(first + i).start())
             spread = []
             wyz = [wy * gz, wy * fz]
             wx = (gx, fx)
@@ -298,16 +349,19 @@
                 for d in range(3):
                     for p in range(2):
                         spread.append(wyz[shift] * (pushes[d] * wx[p]))
-            gsum[...] += lax.dot_general(
-                split(jnp.concatenate(spread, axis=0)),
+            return lax.dot_general(
+                split(jnp.concatenate(spread, axis=0), 0),
                 pick,
                 (((1,), (1,)), ((), ())),
                 preferred_element_type=jnp.float32,
             )
-            return carry
-
-        lax.fori_loop(0, n_trans // per_chunk, chunk, 0)
-        total = gsum[0:96] + gsum[96:192]
+
+        order = (0,) + far_columns[::-1] if step == 0 else far_columns + (0,)
+        total = None
+        for j in order:
+            part = chunk(j)
+            total = part if total is None else total + part
+        total = total[0:96] + total[96:192]
         g = []
         for d in range(3):
             planes = []
@@ -318,12 +372,6 @@
             g.append(jnp.stack(planes))
         return g
 
-    def wait_gather(k, carry):
-        gather_copy(k).wait_recv()
-        return carry
-
-    lax.fori_loop(1, n_trans, wait_gather, 0)
-
     row_of = lax.broadcasted_iota(jnp.int32, (8, 128), 0)
 
     def deep(post):
@@ -334,6 +382,17 @@
             ]
             for i in range(19)
         ]
+
+    def put_row(step, side, at, value):
+        if step < STEPS - 1:
+            ysend[side, 0, at : at + 1, :] = value
+        else:
+            ylast[side, at : at + 1, :] = value
+
+    def got_row(step, side, at):
+        if step < STEPS - 1:
+            return yrecv[side, 0, at : at + 1, :]
+        return ylast_recv[side, at : at + 1, :]
 
     def exchange(step, moved):
         sent = []
@@ -344,11 +403,9 @@
         sent.append(launch(xsend.at[step, 0], xrecv.at[step, 0], x_send.at[step, 0], x_recv.at[step, 0], (s_next, t)))
         sent.append(launch(xsend.at[step, 1], xrecv.at[step, 1], x_send.at[step, 1], x_recv.at[step, 1], (s_prev, t)))
         for q, (i, source, unused) in enumerate(ROWS_UP):
-            ysend[step, UP, q : q + 1, :] = moved[i][source][7:8]
+            put_row(step, UP, q, moved[i][source][7:8])
         for q, (i, source, unused) in enumerate(ROWS_DOWN):
-            ysend[step, DOWN, q : q + 1, :] = moved[i][source][0:1]
-        sent.append(launch(ysend.at[step, UP], yrecv.at[step, UP], y_send.at[step, UP], y_recv.at[step, UP], (s, t_next)))
-        sent.append(launch(ysend.at[step, DOWN], yrecv.at[step, DOWN], y_send.at[step, DOWN], y_recv.at[step, DOWN], (s, t_prev)))
+            put_row(step, DOWN, q, moved[i][source][0:1])
         corner = ((7, 1, 7), (10, 0, 7), (9, 1, 0), (8, 0, 0))
         for q, (i, source, row) in enumerate(corner):
             dsend[step, q] = jnp.broadcast_to(moved[i][source][row : row + 1], (8, 128))
@@ -374,7 +431,7 @@
                             value = flat[row : row + 1]
                         if steep is not None:
                             value = value + steep[inner : inner + 1]
-                        msend[side, p * 4 + m : p * 4 + m + 1, :] = value
+                        ysend[side, 1, p * 4 + m : p * 4 + m + 1, :] = value
                         mine = sum_moment(own, m)
                         mown[side, p * 4 + m : p * 4 + m + 1, :] = (
                             jnp.zeros((1, 128), jnp.float32) if mine is None else mine[7 - row : 8 - row]
@@ -392,10 +449,14 @@
                         if steep is not None:
                             value = value + steep[inner : inner + 1]
                         dsend[step, q, at + m : at + m + 1, :] = value
-            sent.append(launch(msend.at[UP], mrecv.at[UP], m_send.at[UP], m_recv.at[UP], (s, t_next)))
-            sent.append(launch(msend.at[DOWN], mrecv.at[DOWN], m_send.at[DOWN], m_recv.at[DOWN], (s, t_prev)))
         for q, where in enumerate(diagonals):
             sent.append(launch(dsend.at[step, q], drecv.at[step, q], d_send.at[step, q], d_recv.at[step, q], where))
+        for side, where in ((UP, (s, t_next)), (DOWN, (s, t_prev))):
+            if step < STEPS - 1:
+                source, target = ysend.at[side], yrecv.at[side]
+            else:
+                source, target = ylast.at[side], ylast_recv.at[side]
+            sent.append(launch(source, target, y_send.at[step, side], y_recv.at[step, side], where))
         return sent
 
     def sum_moment(members, m):
@@ -421,7 +482,7 @@
                     rows = ROWS_UP if cy == 1 else ROWS_DOWN
                     if source in (0, 1):
                         at = rows.index((i, source, p))
-                        edge = yrecv[step, side, at : at + 1, :]
+                        edge = got_row(step, side, at)
                     else:
                         q = (0 if cx == 1 else 1) + (0 if cy == 1 else 2)
                         at = 4 if cx == 1 else 0
@@ -433,7 +494,7 @@
 
     def edge_moments(step, side):
         low = row_of < 4
-        total = mrecv[side] + mown[side]
+        total = yrecv[side, 1] + mown[side]
         q = 0 if side == UP else 2
         total = total + jnp.where(low, drecv[step, q], drecv[step, q + 1])
         sign = 1 if side == UP else -1
@@ -474,20 +535,6 @@
 
     g = marker_pass(1)
 
-    def return_copy(k):
-        return remote(
-            uret.at[k],
-            urecv.at[k],
-            u_send.at[k],
-            u_recv.at[k],
-            (s, lax.rem(t + n_trans - k, n_trans)),
-        )
-
-    def start_return(k, carry):
-        return_copy(k).start()
-        return carry
-
-    lax.fori_loop(1, n_trans, start_return, 0)
     moved = deep(collide(f, rho, mom, g, solid))
     for copy in exchange(1, moved):
         copy.wait_recv()
@@ -495,46 +542,55 @@
     for i in range(19):
         out_ref[i] = f[i]
 
-    def wait_return(k, carry):
-        return_copy(k).wait_recv()
-        return carry
-
-    lax.fori_loop(1, n_trans, wait_return, 0)
-    vel = uret[0]
-    for k in range(1, n_trans):
-        vel = vel + urecv[k]
-    force_ref[...] = gath[0, 7:8, :] * (gath[0, 4:7, :] - vel[0:3])
+    def others(action):
+        def body(k, carry):
+            pl.when(k != t)(functools.partial(action, k))
+            return carry
+
+        lax.fori_loop(0, n_trans, body, 0)
+
+    urecv[t] = uret[t]
+    others(return_wait)
+    vel = [urecv[k] for k in range(n_trans)]
+    while len(vel) > 1:
+        vel = [vel[k] + vel[k + 1] for k in range(0, len(vel), 2)]
+    force_ref[...] = gath[t, 7:8, :] * (gath[t, 4:7, :] - vel[0][0:3])
 
     for copy in copies:
         copy.wait_send()
 
-    def wait_sends(k, carry):
+    def finish(k):
         gather_copy(k).wait_send()
         return_copy(k).wait_send()
-        return carry
-
-    lax.fori_loop(1, n_trans, wait_sends, 0)
+
+    others(finish)
 
 
 def per_device(n_stream, n_trans, populations, solid, support, fractions, target, area):
-    per_chunk = math.gcd(n_trans, 8)
+    columns = 4 if n_trans % 32 == 0 else 2
+    run = n_trans // columns
     dma = pltpu.SemaphoreType.DMA
     f32 = jnp.float32
     vmem = pl.BlockSpec(memory_space=pltpu.VMEM)
     markers = support.shape[0]
     return pl.pallas_call(
-        functools.partial(kernel, n_stream, n_trans, per_chunk),
+        functools.partial(kernel, n_stream, n_trans, columns),
         out_shape=(
             jax.ShapeDtypeStruct(populations.shape, f32),
             jax.ShapeDtypeStruct((3, markers), f32),
         ),
-        in_specs=[vmem] * 6,
+        in_specs=[pl.BlockSpec(memory_space=pltpu.MemorySpace.HBM)] * 6,
         out_specs=(vmem, vmem),
         scratch_shapes=[
+            pltpu.VMEM(populations.shape, f32),
+            pltpu.VMEM(solid.shape, jnp.int32),
+            pltpu.VMEM((1, markers), jnp.int32),
+            pltpu.VMEM((3, markers), f32),
+            pltpu.VMEM((3, markers), f32),
+            pltpu.VMEM((1, markers), f32),
             pltpu.VMEM((n_trans, 8, 128), f32),
-            pltpu.VMEM((n_trans // per_chunk, 128, per_chunk * 128), jnp.bfloat16),
-            pltpu.VMEM((256, 128), jnp.bfloat16),
-            pltpu.VMEM((192, 128), f32),
+            pltpu.VMEM((columns, 128, run * 128), jnp.bfloat16),
+            pltpu.VMEM((128, 256), jnp.bfloat16),
             pltpu.VMEM((2, 8, 128), f32),
             pltpu.VMEM((2, 8, 128), f32),
             pltpu.VMEM((2, 8, 128), f32),
@@ -549,6 +605,7 @@
             pltpu.VMEM((2, 4, 8, 128), f32),
             pltpu.VMEM((n_trans, 3, 128), f32),
             pltpu.VMEM((n_trans, 3, 128), f32),
+            dma((6,)),
             dma((n_trans,)),
             dma((n_trans,)),
             dma((2,)),
@@ -557,15 +614,13 @@
             dma((2, 2)),
             dma((2, 2)),
             dma((2, 2)),
-            dma((2,)),
-            dma((2,)),
             dma((2, 4)),
             dma((2, 4)),
             dma((n_trans,)),
             dma((n_trans,)),
         ],
         compiler_params=pltpu.CompilerParams(
-            collective_id=0, has_side_effects=True, vmem_limit_bytes=40 * 1024 * 1024
+            collective_id=0, has_side_effects=True, vmem_limit_bytes=56 * 1024 * 1024
         ),
         name="tract",
     )(

time: 61.5 us -> 57.6 us (0.937)
  local copies, waits for them, and re-layouts: 4.2 us -> 2.17 us
  Pallas kernels: 56.4 us -> 54.6 us
    unnamed x14 -> x4, local copies, waits for them, and re-layouts: 4.2 us -> 2.17 us
    pallas_call x1, Pallas kernels: 56.4 us -> 54.6 us  [per_device(): pl.pallas_call(functools.partial(kernel, n_stream, n_trans, columns), out...]
where the time goes in v2:
time: 57.6 us; the launch traced here: 57.4 us
  Pallas kernels  54.6 us (95%)
  local copies, waits for them, and re-layouts  2.17 us (4%)
  between operations  0.65 us (1%)
    pallas_call x1, Pallas kernels, per_device(): pl.pallas_call(functools.partial(kernel, n_stream, n_trans, columns), out...  54.6 us
    unnamed x4, local copies, waits for them, and re-layouts  2.17 us

profile of v2, /device:TPU:1, one launch (start us, length us, event | category | flops | bytes accessed | tf_op | source)
XLA Modules:
  0.0 57.4 jit_solution(17264756807613966386)
XLA Ops:
  0.6 54.6 %tract.1 = (f32[19,2,8,128]{3,2,1,0:T(8,128)}, f32[3,128]{1,0:T(4,128)}) custom-call(f32[19,2,8,128]{3,2,1,0:T(8,128)} %pop_hbm.1, s32[2,8,128]{2,1,0:T(8,128)} %solid_hbm.1, s32[1,128]{1,0:T(1,128)} %bitcast.2, f32[3,128]{1,0:T(4,128)} %frac_hbm.1, f32[3,128]{1,0:T(4,128)} %target_hbm.1, f32[1,128]{1,0:T(1,128)} %bitcast.3), custom_call_target="tpu_custom_call" | custom-call | tf_op jit(solution)/shard_map/tract/pallas_call | solution.py:576
  55.2 0.0 copy-start
  55.3 1.6 %copy.10 = f32[19,2,8,128]{3,2,1,0:T(8,128)} copy(f32[19,2,8,128]{3,2,1,0:T(8,128)} %get-tuple-element.4) | data formatting | bytes 311296
  56.8 0.0 copy-done
  56.8 0.6 %copy.11 = f32[3,128]{1,0:T(4,128)} copy(f32[3,128]{1,0:T(4,128)S(1)} %copy-done) | data formatting | bytes 3072
Async XLA Ops:
  55.2 1.6 %copy-start = (f32[3,128]{1,0:T(4,128)S(1)}, f32[3,128]{1,0:T(4,128)}, u32[]{:S(2)}) copy-start(f32[3,128]{1,0:T(4,128)} %get-tuple-element.5) | copy-start | bytes 4612

commit v3 on v2

--- a/solution.py
+++ b/solution.py
@@ -125,6 +125,7 @@
     vs,
     htile,
     hrecv,
+    wrap,
     hbuf,
     xsend,
     xrecv,
@@ -138,6 +139,11 @@
     uret,
     urecv,
     in_sem,
+    ready,
+    w_send,
+    w_recv,
+    l_send,
+    l_recv,
     g_send,
     g_recv,
     h_send,
@@ -162,9 +168,19 @@
     run = n_trans // columns
     x = t // run
     z = lax.rem(t, run)
-    upper = (2 * z) // run
-    far_first = [upper * q + (1 - upper) * (run - 1 - q) for q in range(run)]
-    far_columns = (2, 1, 3) if columns == 4 else tuple(range(1, columns))
+    own = z * columns + x
+    h = run // 2
+    lower = z < h
+    half = max(n_stream // 2, 1)
+    partners = ((s_next, t), (s_prev, t)) + diagonals + ((s, t_next), (s, t_prev))
+    back = (1, 0, 5, 4, 3, 2, 7, 6)
+
+    def height(where):
+        return (where[0] // half) * run + lax.rem(where[1], run)
+
+    heights = [height(where) for where in partners]
+    level = height((s, t))
+    others_x = (2, 1, 3) if columns == 4 else tuple(range(1, columns))
 
     def column(offset):
         return lax.rem(x + offset, columns)
@@ -182,28 +198,43 @@
             )
         )
     ]
+    for load in loads:
+        load.start()
     barrier = pltpu.get_barrier_semaphore()
 
     def greet(where):
         pl.semaphore_signal(barrier, inc=1, device_id=where, device_id_type=MESH)
 
-    for where in diagonals + ((s_next, t), (s_prev, t)):
-        greet(where)
-    for offset in far_columns:
-        for row in far_first:
-            greet((s, column(offset) * run + row))
-    for row in far_first:
-        pl.when(row != z)(functools.partial(greet, (s, x * run + row)))
-    for load in loads:
-        load.start()
-    for load in loads:
+    expected = jnp.where(lower, h * columns, n_trans) - 1
+    for row in range(run):
+
+        @pl.when(lower | (row >= h))
+        def _():
+            for offset in others_x:
+                greet((s, column(offset) * run + row))
+            pl.when(row != z)(lambda: greet((s, x * run + row)))
+
+    pl.when(z >= h)(lambda: greet((s, t - h)))
+    expected = expected + lower.astype(jnp.int32)
+    if h > 1:
+        pl.when(z == h)(lambda: greet((s, t_prev)))
+        expected = expected + (z == h - 1).astype(jnp.int32)
+    pl.when(z == h)(lambda: greet((s, column(1) * run)))
+    expected = expected + (z == 0).astype(jnp.int32)
+    for where, height_there in zip(partners[:6], heights[:6]):
+        pl.when(height_there >= level)(functools.partial(greet, where))
+        expected = expected + (height_there <= level).astype(jnp.int32)
+
+    for load in loads[1:5]:
         load.wait()
 
-    gath[t, 0:1, :] = support_ref[...].astype(jnp.float32)
-    gath[t, 1:4, :] = frac_ref[...]
-    gath[t, 4:7, :] = target_ref[...]
-    gath[t, 7:8, :] = area_ref[...]
-
+    gath[own, 0:1, :] = support_ref[...].astype(jnp.float32)
+    gath[own, 1:4, :] = frac_ref[...]
+    gath[own, 4:7, :] = target_ref[...]
+    gath[own, 7:8, :] = area_ref[...]
+
+    loads[0].wait()
+    loads[5].wait()
     f = [pop_ref[i] for i in range(19)]
     rho, mom = moments(f)
     inv = 1.0 / rho
@@ -214,7 +245,13 @@
             htile[UP, p * 4 + d : p * 4 + d + 1, :] = ustar[d][p, 7:8, :]
             htile[DOWN, p * 4 + d : p * 4 + d + 1, :] = ustar[d][p, 0:1, :]
 
-    pl.semaphore_wait(barrier, n_trans - 1 + 6)
+    pl.semaphore_wait(barrier, expected)
+
+    def answer(q):
+        pl.semaphore_signal(ready.at[back[q]], inc=1, device_id=partners[q], device_id_type=MESH)
+
+    def await_ready(q):
+        pl.semaphore_wait(ready.at[q], 1)
 
     def remote(src, dst, send, recv, where):
         return pltpu.make_async_remote_copy(
@@ -229,25 +266,64 @@
         copies.append(copy)
         return copy
 
-    halo = [
-        launch(htile.at[UP], hrecv.at[UP], h_send.at[UP], h_recv.at[UP], (s, t_next)),
-        launch(htile.at[DOWN], hrecv.at[DOWN], h_send.at[DOWN], h_recv.at[DOWN], (s, t_prev)),
-    ]
-
-    def gather_copy(k):
-        return remote(gath.at[t], gath.at[t], g_send.at[k], g_recv.at[t], (s, k))
-
-    def gather_wait(k):
-        remote(gath.at[t], gath.at[k], g_send.at[k], g_recv.at[k], (s, k)).wait_recv()
-
-    for offset in far_columns:
-        for row in far_first:
-            gather_copy(column(offset) * run + row).start()
-    for row in far_first:
-        pl.when(row != z)(lambda row=row: gather_copy(x * run + row).start())
-
-    for copy in halo:
-        copy.wait_recv()
+    def tile_copy(where, slot):
+        return remote(gath.at[own], gath.at[own], g_send.at[slot], g_recv.at[own], (s, where))
+
+    def tile_wait(slot):
+        remote(gath.at[own], gath.at[slot], g_send.at[slot], g_recv.at[slot], (s, t_next)).wait_recv()
+
+    def level_copy(row, where, k):
+        part = gath.at[pl.ds(row * columns, columns)]
+        return remote(part, part, l_send.at[k], l_recv.at[row], (s, where))
+
+    def halo_copy(side):
+        where = (s, t_next if side == UP else t_prev)
+        return remote(htile.at[side], hrecv.at[side], h_send.at[side], h_recv.at[side], where)
+
+    def wrap_copy():
+        return remote(
+            htile.at[DOWN], wrap, h_send.at[DOWN], w_recv, (s, column(columns - 1) * run + h)
+        )
+
+    def wrap_on():
+        return remote(wrap, hrecv.at[DOWN], w_send, h_recv.at[DOWN], (s, x * run + run - 1))
+
+    for row in range(run):
+
+        @pl.when((z >= h) | (row < h))
+        def _():
+            for offset in others_x:
+                tile_copy(column(offset) * run + row, row * columns + column(offset)).start()
+            pl.when(row != z)(lambda: tile_copy(x * run + row, row * columns + x).start())
+
+    halo_copy(UP).start()
+    pl.when(z > 0)(lambda: halo_copy(DOWN).start())
+    pl.when(z == 0)(lambda: wrap_copy().start())
+
+    @pl.when(lower)
+    def _():
+        for offset in others_x:
+            tile_wait(z * columns + column(offset))
+        level_copy(z, t + h, z).start()
+
+    for row in range(h):
+
+        @pl.when(row == z - h)
+        def _():
+            level_copy(row, t_next, row).wait_recv()
+            for k in range(h):
+                if k != row:
+                    level_copy(row, x * run + h + k, k).start()
+
+    @pl.when(z == h)
+    def _():
+        wrap_copy().wait_recv()
+        wrap_on().start()
+
+    for q in range(6):
+        pl.when(heights[q] < level)(functools.partial(answer, q))
+    halo_copy(UP).wait_recv()
+    halo_copy(DOWN).wait_recv()
 
     hbuf[...] = jnp.zeros_like(hbuf)
 
@@ -272,25 +348,39 @@
     set_halo(hrecv[UP], hrecv[DOWN])
     set_velocity(ustar)
 
-    width = run * 128
+    tiles = n_trans // columns
+    width = tiles * 128
+    rows_of = tiles // columns
     first_row = (t * 8).astype(jnp.float32)
 
-    def return_copy(k):
-        return remote(uret.at[k], urecv.at[t], u_send.at[k], u_recv.at[t], (s, k))
-
-    def return_wait(k):
-        remote(uret.at[k], urecv.at[k], u_send.at[k], u_recv.at[k], (s, k)).wait_recv()
+    def return_copy(where, slot):
+        return remote(uret.at[slot], urecv.at[own], u_send.at[slot], u_recv.at[own], (s, where))
+
+    def return_wait(slot):
+        remote(uret.at[slot], urecv.at[slot], u_send.at[slot], u_recv.at[slot], (s, t_next)).wait_recv()
 
     def marker_pass(step):
         def chunk(j):
-            first = column(j) * run
+            first = j * tiles
+            rows = range(j * rows_of, (j + 1) * rows_of)
             if step == 0:
-                for i in range(run):
-                    if j:
-                        gather_wait(first + i)
+                for row in rows:
+                    if row < h:
+
+                        @pl.when(lower & (row != z))
+                        def _():
+                            for offset in range(columns):
+                                tile_wait(row * columns + offset)
+
+                        pl.when((z >= h) & (row != z - h))(
+                            lambda: level_copy(row, t_next, 0).wait_recv()
+                        )
                     else:
-                        pl.when(z != i)(functools.partial(gather_wait, first + i))
-            tile = jnp.concatenate([gath[first + i] for i in range(run)], axis=1)
+                        for offset in others_x:
+                            tile_wait(row * columns + column(offset))
+                        pl.when(row != z)(lambda: tile_wait(row * columns + x))
+
+            tile = jnp.concatenate([gath[first + i] for i in range(tiles)], axis=1)
             fx, fy, fz = tile[1:2], tile[2:3], tile[3:4]
             b = jnp.floor(tile[0:1] * (1.0 / 128.0))
             if step == 0:
@@ -333,14 +423,13 @@
             if step == STEPS - 1:
                 mine = (rel >= 0.0) & (rel <= 7.0)
                 for d in range(3):
-                    back = jnp.where(mine, vel[d], 0.0)
-                    for i in range(run):
-                        uret[first + i, d : d + 1, :] = back[:, i * 128 : i * 128 + 128]
-                for i in range(run):
-                    if j:
-                        return_copy(first + i).start()
-                    else:
-                        pl.when(z != i)(lambda i=i: return_copy(first + i).start())
+                    back_to = jnp.where(mine, vel[d], 0.0)
+                    for i in range(tiles):
+                        uret[first + i, d : d + 1, :] = back_to[:, i * 128 : i * 128 + 128]
+                for row in rows:
+                    for offset in others_x:
+                        return_copy(column(offset) * run + row, row * columns + column(offset)).start()
+                    pl.when(row != z)(lambda: return_copy(x * run + row, row * columns + x).start())
             spread = []
             wyz = [wy * gz, wy * fz]
             wx = (gx, fx)
@@ -356,9 +445,8 @@
                 preferred_element_type=jnp.float32,
             )
 
-        order = (0,) + far_columns[::-1] if step == 0 else far_columns + (0,)
         total = None
-        for j in order:
+        for j in range(columns):
             part = chunk(j)
             total = part if total is None else total + part
         total = total[0:96] + total[96:192]
@@ -521,6 +609,8 @@
 
     g = marker_pass(0)
     moved = deep(collide(f, rho, mom, g, solid))
+    for q in range(6):
+        pl.when(heights[q] > level)(functools.partial(await_ready, q))
     for copy in exchange(0, moved):
         copy.wait_recv()
     f = stream(0, moved)
@@ -542,28 +632,38 @@
     for i in range(19):
         out_ref[i] = f[i]
 
+    urecv[own] = uret[own]
+
     def others(action):
-        def body(k, carry):
-            pl.when(k != t)(functools.partial(action, k))
-            return carry
-
-        lax.fori_loop(0, n_trans, body, 0)
-
-    urecv[t] = uret[t]
+        for row in range(run):
+            for offset in others_x:
+                action(row * columns + column(offset))
+            pl.when(row != z)(functools.partial(action, row * columns + x))
+
     others(return_wait)
     vel = [urecv[k] for k in range(n_trans)]
     while len(vel) > 1:
         vel = [vel[k] + vel[k + 1] for k in range(0, len(vel), 2)]
-    force_ref[...] = gath[t, 7:8, :] * (gath[t, 4:7, :] - vel[0][0:3])
+    force_ref[...] = gath[own, 7:8, :] * (gath[own, 4:7, :] - vel[0][0:3])
 
     for copy in copies:
         copy.wait_send()
 
-    def finish(k):
-        gather_copy(k).wait_send()
-        return_copy(k).wait_send()
-
-    others(finish)
+    halo_copy(UP).wait_send()
+    halo_copy(DOWN).wait_send()
+    pl.when(z == h)(lambda: wrap_on().wait_send())
+    for row in range(run):
+
+        @pl.when((z >= h) | (row < h))
+        def _():
+            for offset in others_x:
+                tile_copy(t_next, row * columns + column(offset)).wait_send()
+            pl.when(row != z)(lambda: tile_copy(t_next, row * columns + x).wait_send())
+
+    pl.when(lower)(lambda: level_copy(z, t_next, z).wait_send())
+    for k in range(h):
+        pl.when((z >= h) & (k != z - h))(lambda: level_copy(0, t_next, k).wait_send())
+    others(lambda slot: return_copy(t_next, slot).wait_send())
 
 
 def per_device(n_stream, n_trans, populations, solid, support, fractions, target, area):
@@ -593,6 +693,7 @@
             pltpu.VMEM((128, 256), jnp.bfloat16),
             pltpu.VMEM((2, 8, 128), f32),
             pltpu.VMEM((2, 8, 128), f32),
+            pltpu.VMEM((8, 128), f32),
             pltpu.VMEM((2, 8, 128), f32),
             pltpu.VMEM((2, 2, 5, 8, 128), f32),
             pltpu.VMEM((2, 2, 5, 8, 128), f32),
@@ -606,6 +707,11 @@
             pltpu.VMEM((n_trans, 3, 128), f32),
             pltpu.VMEM((n_trans, 3, 128), f32),
             dma((6,)),
+            pltpu.SemaphoreType.REGULAR((8,)),
+            dma,
+            dma,
+            dma((run,)),
+            dma((run,)),
             dma((n_trans,)),
             dma((n_trans,)),
             dma((2,)),

time: 57.6 us -> 56.4 us (0.979)
  Pallas kernels: 54.6 us -> 53.3 us
    pallas_call x1, Pallas kernels: 54.6 us -> 53.3 us  [per_device(): pl.pallas_call(functools.partial(kernel, n_stream, n_trans, columns), out...]
where the time goes in v3:
time: 56.4 us; the launch traced here: 56.1 us
  Pallas kernels  53.3 us (95%)
  local copies, waits for them, and re-layouts  2.17 us (4%)
  between operations  0.65 us (1%)
    pallas_call x1, Pallas kernels, per_device(): pl.pallas_call(functools.partial(kernel, n_stream, n_trans, columns), out...  53.3 us
    unnamed x4, local copies, waits for them, and re-layouts  2.17 us

profile of v3, /device:TPU:1, one launch (start us, length us, event | category | flops | bytes accessed | tf_op | source)
XLA Modules:
  0.0 56.1 jit_solution(7305989321178355460)
XLA Ops:
  0.6 53.3 %tract.1 = (f32[19,2,8,128]{3,2,1,0:T(8,128)}, f32[3,128]{1,0:T(4,128)}) custom-call(f32[19,2,8,128]{3,2,1,0:T(8,128)} %pop_hbm.1, s32[2,8,128]{2,1,0:T(8,128)} %solid_hbm.1, s32[1,128]{1,0:T(1,128)} %bitcast.2, f32[3,128]{1,0:T(4,128)} %frac_hbm.1, f32[3,128]{1,0:T(4,128)} %target_hbm.1, f32[1,128]{1,0:T(1,128)} %bitcast.3), custom_call_target="tpu_custom_call" | custom-call | tf_op jit(solution)/shard_map/tract/pallas_call | solution.py:676
  53.9 0.0 copy-start
  53.9 1.6 %copy.10 = f32[19,2,8,128]{3,2,1,0:T(8,128)} copy(f32[19,2,8,128]{3,2,1,0:T(8,128)} %get-tuple-element.4) | data formatting | bytes 311296
  55.5 0.0 copy-done
  55.5 0.6 %copy.11 = f32[3,128]{1,0:T(4,128)} copy(f32[3,128]{1,0:T(4,128)S(1)} %copy-done) | data formatting | bytes 3072
Async XLA Ops:
  53.9 1.6 %copy-start = (f32[3,128]{1,0:T(4,128)S(1)}, f32[3,128]{1,0:T(4,128)}, u32[]{:S(2)}) copy-start(f32[3,128]{1,0:T(4,128)} %get-tuple-element.5) | copy-start | bytes 4612

commit v4 on v3

--- a/solution.py
+++ b/solution.py
@@ -258,12 +258,9 @@
             src_ref=src, dst_ref=dst, send_sem=send, recv_sem=recv, device_id=where, device_id_type=MESH
         )
 
-    copies = []
-
     def launch(*args):
         copy = remote(*args)
         copy.start()
-        copies.append(copy)
         return copy
 
     def tile_copy(where, slot):
@@ -426,10 +423,6 @@
                     back_to = jnp.where(mine, vel[d], 0.0)
                     for i in range(tiles):
                         uret[first + i, d : d + 1, :] = back_to[:, i * 128 : i * 128 + 128]
-                for row in rows:
-                    for offset in others_x:
-                        return_copy(column(offset) * run + row, row * columns + column(offset)).start()
-                    pl.when(row != z)(lambda: return_copy(x * run + row, row * columns + x).start())
             spread = []
             wyz = [wy * gz, wy * fz]
             wx = (gx, fx)
@@ -607,11 +600,35 @@
 
     solid = solid_ref[...]
 
+    def others(action):
+        for row in range(run):
+            for offset in others_x:
+                action(row * columns + column(offset))
+            pl.when(row != z)(functools.partial(action, row * columns + x))
+
+    def finish_gather():
+        halo_copy(UP).wait_send()
+        halo_copy(DOWN).wait_send()
+        pl.when(z == h)(lambda: wrap_on().wait_send())
+        for row in range(run):
+
+            @pl.when((z >= h) | (row < h))
+            def _():
+                for offset in others_x:
+                    tile_copy(t_next, row * columns + column(offset)).wait_send()
+                pl.when(row != z)(lambda: tile_copy(t_next, row * columns + x).wait_send())
+
+        pl.when(lower)(lambda: level_copy(z, t_next, z).wait_send())
+        for k in range(h):
+            pl.when((z >= h) & (k != z - h))(lambda: level_copy(0, t_next, k).wait_send())
+
     g = marker_pass(0)
     moved = deep(collide(f, rho, mom, g, solid))
     for q in range(6):
         pl.when(heights[q] > level)(functools.partial(await_ready, q))
-    for copy in exchange(0, moved):
+    first_rims = exchange(0, moved)
+    finish_gather()
+    for copy in first_rims:
         copy.wait_recv()
     f = stream(0, moved)
     low = edge_velocity(edge_moments(0, UP))
@@ -626,44 +643,27 @@
     g = marker_pass(1)
 
     moved = deep(collide(f, rho, mom, g, solid))
-    for copy in exchange(1, moved):
-        copy.wait_recv()
-    f = stream(1, moved)
-    for i in range(19):
-        out_ref[i] = f[i]
-
+    rims = exchange(1, moved)
+    for row in range(run):
+        for offset in others_x:
+            return_copy(column(offset) * run + row, row * columns + column(offset)).start()
+        pl.when(row != z)(lambda: return_copy(x * run + row, row * columns + x).start())
     urecv[own] = uret[own]
-
-    def others(action):
-        for row in range(run):
-            for offset in others_x:
-                action(row * columns + column(offset))
-            pl.when(row != z)(functools.partial(action, row * columns + x))
-
     others(return_wait)
     vel = [urecv[k] for k in range(n_trans)]
     while len(vel) > 1:
         vel = [vel[k] + vel[k + 1] for k in range(0, len(vel), 2)]
     force_ref[...] = gath[own, 7:8, :] * (gath[own, 4:7, :] - vel[0][0:3])
-
-    for copy in copies:
+    for copy in first_rims:
         copy.wait_send()
-
-    halo_copy(UP).wait_send()
-    halo_copy(DOWN).wait_send()
-    pl.when(z == h)(lambda: wrap_on().wait_send())
-    for row in range(run):
-
-        @pl.when((z >= h) | (row < h))
-        def _():
-            for offset in others_x:
-                tile_copy(t_next, row * columns + column(offset)).wait_send()
-            pl.when(row != z)(lambda: tile_copy(t_next, row * columns + x).wait_send())
-
-    pl.when(lower)(lambda: level_copy(z, t_next, z).wait_send())
-    for k in range(h):
-        pl.when((z >= h) & (k != z - h))(lambda: level_copy(0, t_next, k).wait_send())
     others(lambda slot: return_copy(t_next, slot).wait_send())
+    for copy in rims:
+        copy.wait_recv()
+    f = stream(1, moved)
+    for i in range(19):
+        out_ref[i] = f[i]
+    for copy in rims:
+        copy.wait_send()
 
 
 def per_device(n_stream, n_trans, populations, solid, support, fractions, target, area):

time: 56.4 us -> 56.1 us (level)
  no operation moved by 1% of the time
where the time goes in v4:
time: 56.1 us; the launch traced here: 55.9 us
  Pallas kernels  53.1 us (95%)
  local copies, waits for them, and re-layouts  2.17 us (4%)
  between operations  0.65 us (1%)
    pallas_call x1, Pallas kernels, per_device(): pl.pallas_call(functools.partial(kernel, n_stream, n_trans, columns), out...  53.1 us
    unnamed x4, local copies, waits for them, and re-layouts  2.17 us

profile of v4, /device:TPU:1, one launch (start us, length us, event | category | flops | bytes accessed | tf_op | source)
XLA Modules:
  0.0 55.9 jit_solution(3526503543320083217)
XLA Ops:
  0.6 53.1 %tract.1 = (f32[19,2,8,128]{3,2,1,0:T(8,128)}, f32[3,128]{1,0:T(4,128)}) custom-call(f32[19,2,8,128]{3,2,1,0:T(8,128)} %pop_hbm.1, s32[2,8,128]{2,1,0:T(8,128)} %solid_hbm.1, s32[1,128]{1,0:T(1,128)} %bitcast.2, f32[3,128]{1,0:T(4,128)} %frac_hbm.1, f32[3,128]{1,0:T(4,128)} %target_hbm.1, f32[1,128]{1,0:T(1,128)} %bitcast.3), custom_call_target="tpu_custom_call" | custom-call | tf_op jit(solution)/shard_map/tract/pallas_call | solution.py:676
  53.7 0.0 copy-start
  53.8 1.6 %copy.10 = f32[19,2,8,128]{3,2,1,0:T(8,128)} copy(f32[19,2,8,128]{3,2,1,0:T(8,128)} %get-tuple-element.4) | data formatting | bytes 311296
  55.3 0.0 copy-done
  55.3 0.6 %copy.11 = f32[3,128]{1,0:T(4,128)} copy(f32[3,128]{1,0:T(4,128)S(1)} %copy-done) | data formatting | bytes 3072
Async XLA Ops:
  53.7 1.6 %copy-start = (f32[3,128]{1,0:T(4,128)S(1)}, f32[3,128]{1,0:T(4,128)}, u32[]{:S(2)}) copy-start(f32[3,128]{1,0:T(4,128)} %get-tuple-element.5) | copy-start | bytes 4612

commit v5 on v4

--- a/solution.py
+++ b/solution.py
@@ -285,6 +285,10 @@
     def wrap_on():
         return remote(wrap, hrecv.at[DOWN], w_send, h_recv.at[DOWN], (s, x * run + run - 1))
 
+    halo_copy(UP).start()
+    pl.when(z > 0)(lambda: halo_copy(DOWN).start())
+    pl.when(z == 0)(lambda: wrap_copy().start())
+
     for row in range(run):
 
         @pl.when((z >= h) | (row < h))
@@ -292,10 +296,6 @@
             for offset in others_x:
                 tile_copy(column(offset) * run + row, row * columns + column(offset)).start()
             pl.when(row != z)(lambda: tile_copy(x * run + row, row * columns + x).start())
-
-    halo_copy(UP).start()
-    pl.when(z > 0)(lambda: halo_copy(DOWN).start())
-    pl.when(z == 0)(lambda: wrap_copy().start())
 
     @pl.when(lower)
     def _():

time: 56.1 us -> 56 us (level)
  no operation moved by 1% of the time
where the time goes in v5:
time: 56 us; the launch traced here: 55.8 us
  Pallas kernels  53 us (95%)
  local copies, waits for them, and re-layouts  2.17 us (4%)
  between operations  0.65 us (1%)
    pallas_call x1, Pallas kernels, per_device(): pl.pallas_call(functools.partial(kernel, n_stream, n_trans, columns), out...  53 us
    unnamed x4, local copies, waits for them, and re-layouts  2.17 us

profile of v5, /device:TPU:1, one launch (start us, length us, event | category | flops | bytes accessed | tf_op | source)
XLA Modules:
  0.0 55.8 jit_solution(1978895386189895577)
XLA Ops:
  0.6 53.0 %tract.1 = (f32[19,2,8,128]{3,2,1,0:T(8,128)}, f32[3,128]{1,0:T(4,128)}) custom-call(f32[19,2,8,128]{3,2,1,0:T(8,128)} %pop_hbm.1, s32[2,8,128]{2,1,0:T(8,128)} %solid_hbm.1, s32[1,128]{1,0:T(1,128)} %bitcast.2, f32[3,128]{1,0:T(4,128)} %frac_hbm.1, f32[3,128]{1,0:T(4,128)} %target_hbm.1, f32[1,128]{1,0:T(1,128)} %bitcast.3), custom_call_target="tpu_custom_call" | custom-call | tf_op jit(solution)/shard_map/tract/pallas_call | solution.py:676
  53.7 0.0 copy-start
  53.7 1.6 %copy.10 = f32[19,2,8,128]{3,2,1,0:T(8,128)} copy(f32[19,2,8,128]{3,2,1,0:T(8,128)} %get-tuple-element.4) | data formatting | bytes 311296
  55.3 0.0 copy-done
  55.3 0.6 %copy.11 = f32[3,128]{1,0:T(4,128)} copy(f32[3,128]{1,0:T(4,128)S(1)} %copy-done) | data formatting | bytes 3072
Async XLA Ops:
  53.7 1.6 %copy-start = (f32[3,128]{1,0:T(4,128)S(1)}, f32[3,128]{1,0:T(4,128)}, u32[]{:S(2)}) copy-start(f32[3,128]{1,0:T(4,128)} %get-tuple-element.5) | copy-start | bytes 4612

commit v6 on v5

--- a/solution.py
+++ b/solution.py
@@ -356,27 +356,26 @@
     def return_wait(slot):
         remote(uret.at[slot], urecv.at[slot], u_send.at[slot], u_recv.at[slot], (s, t_next)).wait_recv()
 
+    def await_tiles(row, offsets):
+        for offset in offsets:
+            tile_wait(row * columns + column(offset))
+
+    def await_row(row, own_half):
+        if own_half:
+            pl.when(row != z)(lambda: await_tiles(row, range(columns)))
+            pl.when((row == z) & (z >= h))(lambda: await_tiles(row, others_x))
+        else:
+            pl.when(lower)(lambda: await_tiles(row, range(columns)))
+            pl.when((z >= h) & (row != z - h))(lambda: level_copy(row, t_next, 0).wait_recv())
+
     def marker_pass(step):
         def chunk(j):
-            first = j * tiles
-            rows = range(j * rows_of, (j + 1) * rows_of)
+            at = j
             if step == 0:
-                for row in rows:
-                    if row < h:
-
-                        @pl.when(lower & (row != z))
-                        def _():
-                            for offset in range(columns):
-                                tile_wait(row * columns + offset)
-
-                        pl.when((z >= h) & (row != z - h))(
-                            lambda: level_copy(row, t_next, 0).wait_recv()
-                        )
-                    else:
-                        for offset in others_x:
-                            tile_wait(row * columns + column(offset))
-                        pl.when(row != z)(lambda: tile_wait(row * columns + x))
-
+                at = jnp.where(lower, j, columns - 1 - j)
+                for k in range(rows_of):
+                    await_row(at * rows_of + k, j < columns // 2)
+            first = at * tiles
             tile = jnp.concatenate([gath[first + i] for i in range(tiles)], axis=1)
             fx, fy, fz = tile[1:2], tile[2:3], tile[3:4]
             b = jnp.floor(tile[0:1] * (1.0 / 128.0))
@@ -384,9 +383,9 @@
                 e = tile[0:1] - 128.0 * b
                 depth = lax.broadcasted_iota(jnp.int32, (128, width), 0).astype(jnp.float32)
                 pick = jnp.where(depth == e, 1.0, 0.0).astype(jnp.bfloat16)
-                onehot[j] = pick
+                onehot[at] = pick
             else:
-                pick = onehot[j]
+                pick = onehot[at]
             r = lax.dot_general(
                 vs[...],
                 jnp.concatenate([pick, pick], axis=0),

time: 56 us -> 56 us (level)
  no operation moved by 1% of the time
where the time goes in v6:
time: 56 us; the launch traced here: 55.8 us
  Pallas kernels  53 us (95%)
  local copies, waits for them, and re-layouts  2.17 us (4%)
  between operations  0.65 us (1%)
    pallas_call x1, Pallas kernels, per_device(): pl.pallas_call(functools.partial(kernel, n_stream, n_trans, columns), out...  53 us
    unnamed x4, local copies, waits for them, and re-layouts  2.17 us

profile of v6, /device:TPU:1, one launch (start us, length us, event | category | flops | bytes accessed | tf_op | source)
XLA Modules:
  0.0 55.8 jit_solution(9387963991909009120)
XLA Ops:
  0.6 53.0 %tract.1 = (f32[19,2,8,128]{3,2,1,0:T(8,128)}, f32[3,128]{1,0:T(4,128)}) custom-call(f32[19,2,8,128]{3,2,1,0:T(8,128)} %pop_hbm.1, s32[2,8,128]{2,1,0:T(8,128)} %solid_hbm.1, s32[1,128]{1,0:T(1,128)} %bitcast.2, f32[3,128]{1,0:T(4,128)} %frac_hbm.1, f32[3,128]{1,0:T(4,128)} %target_hbm.1, f32[1,128]{1,0:T(1,128)} %bitcast.3), custom_call_target="tpu_custom_call" | custom-call | tf_op jit(solution)/shard_map/tract/pallas_call | solution.py:675
  53.7 0.0 copy-start
  53.7 1.6 %copy.10 = f32[19,2,8,128]{3,2,1,0:T(8,128)} copy(f32[19,2,8,128]{3,2,1,0:T(8,128)} %get-tuple-element.4) | data formatting | bytes 311296
  55.3 0.0 copy-done
  55.3 0.6 %copy.11 = f32[3,128]{1,0:T(4,128)} copy(f32[3,128]{1,0:T(4,128)S(1)} %copy-done) | data formatting | bytes 3072
Async XLA Ops:
  53.7 1.6 %copy-start = (f32[3,128]{1,0:T(4,128)S(1)}, f32[3,128]{1,0:T(4,128)}, u32[]{:S(2)}) copy-start(f32[3,128]{1,0:T(4,128)} %get-tuple-element.5) | copy-start | bytes 4612
